TPU v7x, 512 devices: a whole 4x8x8 slice. The times are simulated.
512 devices in a mesh: tm: 16 (over z_hi, x), spin: 32 (over z_lo, y, core).
Axes of the slice: x: 4, y: 8, z: 8 (z_hi: 4, z_lo: 2; z = z_hi * 2 + z_lo), core: 2. Of those that a mesh axis runs over, the one named last changes fastest.
Arguments:
- strain: float32 [4, 131072], P(None, ('tm', 'spin')), may hold values from -6 to 6
- stencil_start: int32 [16, 1024], P(None, 'tm'), may hold values from -64 to 64
- stencil_frac: float32 [16, 1024], P(None, 'tm'), may hold values from 0 to 1
- antenna: float32 [2, 16, 2, 131072], P(None, None, None, ('tm', 'spin')), may hold values from -10 to 10
- spin_index: int32 [128], P('spin'), may hold values from 0 to 511
Outputs:
- fstat: float32 [128, 16, 256], P('spin', None, 'tm')
All inputs are finite; a program needn't handle non-finite values.
Results may differ from a plain program's by a relative error of at most 0.0003.
The roundings to bfloat16 on the way count: a program that leaves them out, or rounds other values in their place, can miss the bound.
Values may be sent and summed in bfloat16 or wider, within the bound.
A program may use at most 64 MiB of HBM per device.

v0:
```python
import math

import jax
import jax.numpy as jnp
from jax import lax
from jax.sharding import PartitionSpec as P

NF = 256
BLK = 128
SHIFT_MAX = 64


chirp_rate = 0.015625
full_turn = 2.0 * math.pi
norm_floor = 1e-06
piece_limit = 1024
coarse_step = 8


def padded_2(value, sides, width):
    for axis, dim in sides:
        count, length = (lax.axis_size(axis), value.shape[dim])
        up = [(i, (i + 1) % count) for i in range(count - 1)]
        down = [(j, i) for i, j in up]
        last = lax.slice_in_dim(value, length - width, length, axis=dim)
        first = lax.slice_in_dim(value, 0, width, axis=dim)
        before = lax.ppermute(last, axis, up)
        after = lax.ppermute(first, axis, down)
        value = jnp.concatenate([before, value, after], axis=dim)
    return value


def lagrange_weights(fraction):
    upper_term = fraction + 1.0
    lower_term = fraction - 1.0
    further_term = fraction - 2.0
    return (
        -fraction * lower_term * further_term / 6.0,
        upper_term * lower_term * further_term / 2.0,
        -upper_term * fraction * further_term / 2.0,
        upper_term * fraction * lower_term / 6.0,
    )


def resample(padded, starts, fractions, margin, block_len):
    row_count = padded.shape[0]
    patch_count = starts.shape[0]
    sample_count = padded.shape[1] - 2 * margin
    block_count = sample_count // block_len
    reach = 2 * (margin - 2)
    span = block_len + reach + 2 * coarse_step
    pieces = -(-span // block_len)
    tail = padded[:, 1:]
    extended = jnp.pad(tail, ((0, 0), (0, (block_count + pieces) * block_len - tail.shape[1])))
    blocked = extended.reshape(row_count, block_count + pieces, block_len)
    windows = jnp.concatenate(
        [blocked[:, index : index + block_count] for index in range(pieces)], axis=2
    )
    shift = starts + (margin - 2)
    coarse = shift // coarse_step
    fine = shift - coarse_step * coarse
    wide = block_len + 2 * coarse_step
    picked = jnp.zeros((row_count, patch_count, block_count, wide), jnp.float32)
    for level in range(reach // coarse_step + 1):
        chosen = (coarse == level)[None, :, :, None]
        window_part = windows[:, None, :, coarse_step * level : coarse_step * level + wide]
        picked = jnp.where(chosen, window_part, picked)
    weights = lagrange_weights(fractions)
    result = jnp.zeros((row_count, patch_count, block_count, block_len), jnp.float32)
    for offset in range(coarse_step + 3):
        factor = jnp.zeros(starts.shape, jnp.float32)
        for stencil_tap in range(4):
            factor = factor + jnp.where(fine + stencil_tap == offset, weights[stencil_tap], 0.0)
        result = result + factor[None, :, :, None] * picked[..., offset : offset + block_len]
    return result.reshape(row_count, patch_count, sample_count)


def apply_antenna(resampled, antenna):
    series = []
    for pattern in range(2):
        for column in range(2):
            series.append(
                antenna[pattern, :, 0, :] * resampled[column]
                + antenna[pattern, :, 1, :] * resampled[2 + column]
            )
    return jnp.stack(series, axis=1).astype(jnp.bfloat16)


def dft_table(local_time, total_len, nbins):
    bin_index = jnp.arange(nbins, dtype=jnp.int32)
    angles = (
        full_turn
        * (local_time[:, None] * bin_index[None, :] % total_len).astype(jnp.float32)
        / total_len
    )
    return jnp.concatenate([jnp.cos(angles), jnp.sin(angles)], axis=1).astype(jnp.bfloat16)


def spectra_terms(segment, local_start, anchor, spin_index, total_len, nbins):
    length = segment.shape[2]
    local_time = local_start + jnp.arange(length, dtype=jnp.int32)
    scaled = (anchor + local_time).astype(jnp.float32) / total_len
    cycles = spin_index.astype(jnp.float32)[:, None] * chirp_rate * (scaled * scaled)[None, :]
    phase = full_turn * (cycles - jnp.floor(cycles))
    cosine = jnp.cos(phase)[:, None, None, :]
    sine = jnp.sin(phase)[:, None, None, :]
    values = segment.astype(jnp.float32)
    real_part = values[:, 0::2][None]
    imag_part = values[:, 1::2][None]
    demod_real = real_part * cosine + imag_part * sine
    demod_imag = imag_part * cosine - real_part * sine
    demodulated = (
        jnp.stack([demod_real, demod_imag], axis=3)
        .reshape(spin_index.shape[0], segment.shape[0], 4, length)
        .astype(jnp.bfloat16)
    )
    table = dft_table(local_time, total_len, nbins)
    product = jnp.dot(demodulated.reshape(-1, length), table, preferred_element_type=jnp.float32)
    return product.reshape(spin_index.shape[0], segment.shape[0], 4, 2 * nbins)


def spectra_fold(running, piece, start, anchor, spin_index, total_len, nbins):
    length = piece.shape[2]
    step_len = max(
        (divisor for divisor in range(1, min(length, piece_limit) + 1) if length % divisor == 0)
    )

    def add_step(turn_index, accum):
        segment = lax.dynamic_slice_in_dim(piece, turn_index * step_len, step_len, 2)
        return accum + spectra_terms(
            segment, start + turn_index * step_len, anchor, spin_index, total_len, nbins
        )

    return lax.fori_loop(0, length // step_len, add_step, running)


def block_spectra(sums, anchor, total_len, nbins):
    with_cos = sums[..., :nbins]
    with_sin = sums[..., nbins:]
    part_real = with_cos[:, :, 0::2] + with_sin[:, :, 1::2]
    part_imag = with_cos[:, :, 1::2] - with_sin[:, :, 0::2]
    bin_index = jnp.arange(nbins, dtype=jnp.int32)
    angles = full_turn * (bin_index * anchor % total_len).astype(jnp.float32) / total_len
    cos_block = jnp.cos(angles)
    sin_block = jnp.sin(angles)
    shifted_real = part_real * cos_block + part_imag * sin_block
    shifted_imag = part_imag * cos_block - part_real * sin_block
    stacked = jnp.stack([shifted_real, shifted_imag], axis=3)
    return stacked.reshape(sums.shape[0], sums.shape[1], 4, nbins)


def statistic(spectra, norms):
    squares = spectra * spectra
    return (squares[:, :, 0] + squares[:, :, 1]) / norms[0][None, :, None] + (
        squares[:, :, 2] + squares[:, :, 3]
    ) / norms[1][None, :, None]


def body(strain, stencil_start, stencil_frac, antenna, spin_index):
    own_len = strain.shape[1]
    tm_count = lax.axis_size("tm")
    spin_count = lax.axis_size("spin")
    block_total = own_len * spin_count
    total_len = block_total * tm_count
    margin = SHIFT_MAX + 2
    anchor = lax.axis_index("tm") * block_total
    empty_sums = jnp.zeros((spin_index.shape[0], antenna.shape[1], 4, 2 * NF), jnp.float32)
    norms = lax.psum(jnp.sum(antenna * antenna, axis=(2, 3)), ("tm", "spin")) + norm_floor
    block_strain, block_antenna = (
        lax.all_gather(strain, "spin", axis=1, tiled=True),
        lax.all_gather(antenna.reshape(-1, own_len), "spin", axis=1, tiled=True),
    )
    padded = padded_2(block_strain, (("tm", 1),), margin)
    resampled = resample(padded, stencil_start, stencil_frac, margin, BLK)
    weighted = apply_antenna(resampled, block_antenna.reshape(2, antenna.shape[1], 2, block_total))
    sums = spectra_fold(empty_sums, weighted, 0, anchor, spin_index, total_len, NF)
    partial_spectra = block_spectra(sums, anchor, total_len, NF)
    summed = lax.psum(partial_spectra, "tm")
    share_len = NF // tm_count
    summed = lax.dynamic_slice_in_dim(summed, lax.axis_index("tm") * share_len, share_len, 3)
    return statistic(summed, norms)


def solution(mesh):
    return jax.shard_map(
        body,
        mesh=mesh,
        in_specs=(
            P(None, ("tm", "spin")),
            P(None, "tm"),
            P(None, "tm"),
            P(None, None, None, ("tm", "spin")),
            P("spin"),
        ),
        out_specs=P("spin", None, "tm"),
        check_vma=False,
    )
```

profile of v0, /device:TPU:24, one launch (start us, length us, event | category | flops | bytes accessed | tf_op | source)
XLA Modules:
  0.0 405.9 jit_solution(8161924389470855618)
XLA Ops:
  6.5 1.5 reshape.365
  8.1 33.5 %all_gather.7 = f32[4,8192]{1,0:T(4,128)S(1)} all-gather(f32[4,256]{1,0:T(4,128)} %param.7), channel_id=1, replica_groups=mesh['tm'=16,'spin'=32] {'spin'}, dimensions={1}, use_global_device_ids=true | all-gather | bytes 135168 | tf_op jit(solution)/shard_map/all_gather | solution.py:170
  41.6 0.1 fusion.59
  41.7 1.3 collective-permute-start
  43.0 1.3 collective-permute-start.1
  44.3 1.0 multiply_reduce_fusion
  45.3 0.7 convert_bitcast_fusion
  46.0 0.7 select_add_fusion.10
  46.8 0.7 select_add_fusion.9
  47.6 105.5 %psum.15 = f32[2,16]{1,0:T(2,128)S(1)} all-reduce(f32[2,16]{1,0:T(2,128)S(1)} %multiply_reduce_fusion), channel_id=1, replica_groups=mesh['tm'=16,'spin'=32] {'tm','spin'}, use_global_device_ids=true, to_apply=%region_4.5 | all-reduce | flops 32 | bytes 256 | tf_op jit(solution)/shard_map/psum | solution.py:168
  153.0 0.2 concatenate.37
  153.3 0.1 slice.269
  153.4 0.1 reshape.367
  153.5 0.8 fusion.30
  154.3 0.9 pad_maximum_fusion.5
  155.2 6.8 %select_select_fusion = f32[4,16,64,144]{3,2,1,0:T(8,128)S(1)} fusion(f32[4,64,144]{2,1,0:T(8,128)S(1)} %get-tuple-element.216, f32[4,64,144]{2,1,0:T(8,128)S(1)} %get-tuple-element.215, f32[4,64,144]{2,1,0:T(8,128)S(1)} %get-tuple-element.214, f32[4,64,144]{2,1,0:T(8,128)S(1)} %get-tuple-element.213, f32[4,64,144]{2,1,0:T(8,128)S(1)} %get-tuple-element.212, ...), kind=kLoop, calls=%fused_computation.28 | loop fusion | flops 10027008 | bytes 4883456 | tf_op jit(solution)/shard_map/jit(_where)/select_n | solution.py:67
  162.0 7.2 %fusion.12 = f32[4,16,64,128]{3,2,1,0:T(8,128)S(1)} fusion(f32[4,16,64,144]{3,2,1,0:T(8,128)S(1)} %select_select_fusion, f32[16,64]{1,0:T(8,128)S(1)} %get-tuple-element.229, f32[16,64]{1,0:T(8,128)S(1)} %get-tuple-element.228, f32[16,64]{1,0:T(8,128)S(1)} %get-tuple-element.230, f32[16,64]{1,0:T(8,128)S(1)} %get-tuple-element.231, ...), kind=kLoop, calls=%fused_computation.30 | loop fusion | flops 11010048 | bytes 25210880 | tf_op jit(solution)/shard_map/add | solution.py:74
  169.3 1.1 fusion.56
  170.4 2.5 reshape.366
  172.9 4.2 %add_convert_fusion.4 = (bf16[16,1,8192]{2,1,0:T(2,128)(2,1)S(1)}, bf16[16,1,8192]{2,1,0:T(2,128)(2,1)S(1)}, bf16[16,1,8192]{2,1,0:T(2,128)(2,1)S(1)}, bf16[16,1,8192]{2,1,0:T(2,128)(2,1)S(1)}) fusion(f32[16,1,8192]{2,1,0:T(1,128)} %bitcast.72, f32[16,1,8192]{2,1,0:T(1,128)S(1)} %bitcast.69, f32[2,16,2,8192]{3,2,1,0:T(2,128)S(1)} %reshape.366, ...), kind=kLoop, calls=%fused_computation.86 | loop fusion | flops 2097152 | bytes 5242880 | tf_op jit(solution)/shard_map/convert.4
  177.1 2.4 pad_maximum_fusion.1
  179.6 48.7 %while.16 = (s32[]{:T(128)}, f32[4,16,4,512]{3,1,2,0:T(8,128)S(1)}, bf16[16,4,8192]{2,1,0:T(4,128)(2,1)S(1)}, f32[4,1]{0,1:T(1,128)S(1)}, s32[]{:T(128)}, /*index=5*/s32[]{:T(128)}, s32[]{:T(128)}, s32[]{:T(128)}, s32[]{:T(128)}) while((s32[]{:T(128)}, f32[4,16,4,512]{3,1,2,0:T(8,128)S(1)}, bf16[16,4,8192]{2,1,0:T(4,128)(2,1)S(1)}, ...), condition=%wide.region_1.0_spmd.clone, body=%wide.region_0.0_spmd.clone.sunk | while | flops 276387840 | bytes 6766805 | solution.py:134
  179.6 0.1 constant_dynamic-slice_fusion.2
  179.8 0.2 fusion.65
  180.0 0.1 add_convert_fusion.6
  180.2 5.0 %cosine_convert_fusion.2 = (bf16[1024,256]{1,0:T(8,128)(2,1)S(1)}, bf16[1024,256]{1,0:T(8,128)(2,1)S(1)}) fusion(s32[1024]{0:T(1024)S(1)} %iota_add_fusion.2), kind=kLoop, calls=%fused_computation.11.clone.1 | loop fusion | flops 4194304 | bytes 1052672 | tf_op jit(solution)/shard_map/convert
  185.2 0.5 convolution_add_fusion.2
  185.7 0.1 constant_dynamic-slice_fusion.2
  185.9 0.2 fusion.65
  186.1 0.1 add_convert_fusion.6
  186.3 5.0 %cosine_convert_fusion.2 = (bf16[1024,256]{1,0:T(8,128)(2,1)S(1)}, bf16[1024,256]{1,0:T(8,128)(2,1)S(1)}) fusion(s32[1024]{0:T(1024)S(1)} %iota_add_fusion.2), kind=kLoop, calls=%fused_computation.11.clone.1 | loop fusion | flops 4194304 | bytes 1052672 | tf_op jit(solution)/shard_map/convert
  191.2 0.5 convolution_add_fusion.2
  191.8 0.1 constant_dynamic-slice_fusion.2
  191.9 0.2 fusion.65
  192.1 0.1 add_convert_fusion.6
  192.4 5.0 %cosine_convert_fusion.2 = (bf16[1024,256]{1,0:T(8,128)(2,1)S(1)}, bf16[1024,256]{1,0:T(8,128)(2,1)S(1)}) fusion(s32[1024]{0:T(1024)S(1)} %iota_add_fusion.2), kind=kLoop, calls=%fused_computation.11.clone.1 | loop fusion | flops 4194304 | bytes 1052672 | tf_op jit(solution)/shard_map/convert
  197.3 0.5 convolution_add_fusion.2
  198.0 0.2 fusion.65
  198.2 0.1 add_convert_fusion.6
  198.4 5.0 %cosine_convert_fusion.2 = (bf16[1024,256]{1,0:T(8,128)(2,1)S(1)}, bf16[1024,256]{1,0:T(8,128)(2,1)S(1)}) fusion(s32[1024]{0:T(1024)S(1)} %iota_add_fusion.2), kind=kLoop, calls=%fused_computation.11.clone.1 | loop fusion | flops 4194304 | bytes 1052672 | tf_op jit(solution)/shard_map/convert
  203.4 0.5 convolution_add_fusion.2
  203.9 0.1 constant_dynamic-slice_fusion.2
  204.1 0.2 fusion.65
  204.3 0.1 add_convert_fusion.6
  204.5 5.0 %cosine_convert_fusion.2 = (bf16[1024,256]{1,0:T(8,128)(2,1)S(1)}, bf16[1024,256]{1,0:T(8,128)(2,1)S(1)}) fusion(s32[1024]{0:T(1024)S(1)} %iota_add_fusion.2), kind=kLoop, calls=%fused_computation.11.clone.1 | loop fusion | flops 4194304 | bytes 1052672 | tf_op jit(solution)/shard_map/convert
  209.5 0.5 convolution_add_fusion.2
  210.2 0.2 fusion.65
  210.4 0.1 add_convert_fusion.6
  210.6 5.0 %cosine_convert_fusion.2 = (bf16[1024,256]{1,0:T(8,128)(2,1)S(1)}, bf16[1024,256]{1,0:T(8,128)(2,1)S(1)}) fusion(s32[1024]{0:T(1024)S(1)} %iota_add_fusion.2), kind=kLoop, calls=%fused_computation.11.clone.1 | loop fusion | flops 4194304 | bytes 1052672 | tf_op jit(solution)/shard_map/convert
  215.6 0.5 convolution_add_fusion.2
  216.1 0.1 constant_dynamic-slice_fusion.2
  216.3 0.2 fusion.65
  216.5 0.1 add_convert_fusion.6
  216.7 5.0 %cosine_convert_fusion.2 = (bf16[1024,256]{1,0:T(8,128)(2,1)S(1)}, bf16[1024,256]{1,0:T(8,128)(2,1)S(1)}) fusion(s32[1024]{0:T(1024)S(1)} %iota_add_fusion.2), kind=kLoop, calls=%fused_computation.11.clone.1 | loop fusion | flops 4194304 | bytes 1052672 | tf_op jit(solution)/shard_map/convert
  221.7 0.5 convolution_add_fusion.2
  222.2 0.1 constant_dynamic-slice_fusion.2
  222.4 0.2 fusion.65
  222.6 0.1 add_convert_fusion.6
  222.8 5.0 %cosine_convert_fusion.2 = (bf16[1024,256]{1,0:T(8,128)(2,1)S(1)}, bf16[1024,256]{1,0:T(8,128)(2,1)S(1)}) fusion(s32[1024]{0:T(1024)S(1)} %iota_add_fusion.2), kind=kLoop, calls=%fused_computation.11.clone.1 | loop fusion | flops 4194304 | bytes 1052672 | tf_op jit(solution)/shard_map/convert
  227.8 0.5 convolution_add_fusion.2
  228.4 0.7 copy.8
  229.2 168.2 %all-reduce.3.cloned.1.call-done = f32[4,16,4,256]{3,1,0,2:T(8,128)} async-done(((f32[4,16,4,256]{3,1,0,2:T(8,128)}), f32[4,16,4,256]{3,1,0,2:T(8,128)}) %all-reduce.3.cloned.1.call-update) | async-done | bytes 262160 | tf_op jit(solution)/shard_map/psum | solution.py:178
  397.3 1.0 dynamic-slice_multiply_fusion
  398.3 0.7 fusion.38
  (69 shorter events, 1.5 us)
Async XLA Ops:
  6.5 163.9 %all-gather.2.cloned.1.call-start = ((), (), s32[]{:S(2)}) async-start(), calls=%async_computation | async-start | bytes 2162688 | tf_op jit(solution)/shard_map/all_gather | solution.py:171
  8.1 389.3 %all-reduce.3.cloned.1.call-start = ((), (), s32[]{:S(2)}) async-start(), calls=%async_computation.1 | async-start | bytes 524288 | tf_op jit(solution)/shard_map/psum | solution.py:178
  41.7 111.4 %collective-permute-start = (f32[4,66]{1,0:T(4,128)S(1)}, f32[4,66]{1,0:T(4,128)S(1)}, u32[]{:S(2)}, u32[]{:S(2)}) collective-permute-start(f32[4,66]{1,0:T(4,128)S(1)} %get-tuple-element.221), channel_id=1, source_target_pairs={{0,32},{32,64},{64,96},{96,128},{128,160},{160,192},{192,224},{224... | collective-permute-start | bytes 3176 | tf_op jit(solution)/shard_map/ppermute | solution.py:27
  43.0 110.1 %collective-permute-start.1 = (f32[4,66]{1,0:T(4,128)S(1)}, f32[4,66]{1,0:T(4,128)S(1)}, u32[]{:S(2)}, u32[]{:S(2)}) collective-permute-start(f32[4,66]{1,0:T(4,128)S(1)} %get-tuple-element.220), channel_id=1, source_target_pairs={{32,0},{64,32},{96,64},{128,96},{160,128},{192,160},{224,192},{256... | collective-permute-start | bytes 3176 | tf_op jit(solution)/shard_map/ppermute | solution.py:28
  177.1 2.5 copy-start
Sparse Core Ops, SparseCore 0:
  9.5 70.3 all-gather.1
  229.3 168.0 all-reduce.2
where the time goes:
time: 407 us; the launch traced here: 406 us
  waiting for transfers between devices  168 us (41%)
  blocking collectives  139 us (34%)
  other arithmetic  70.7 us (17%)
  between operations  13.6 us (3%)
  local copies, waits for them, and re-layouts  6.98 us (2%)
    psum x1, waiting for transfers between devices, body(): summed = lax.psum(partial_spectra, 'tm')  168 us
    psum x1, blocking collectives, body(): lax.psum(jnp.sum(antenna * antenna, axis=(2, 3)), ('tm', 'spin'))  105 us
    another operation x17, other arithmetic  45 us
    all_gather x1, blocking collectives, body(): lax.all_gather(strain, 'spin', axis=1, tiled=True)  33.5 us
  transfers between devices with their start and end apart: 4, of which 1 were waited for; matrix products, arithmetic and copies ran while one was open for 5% of the time, Pallas kernels for 0%

commit v1 on v0

v1 whole, which is shorter than its diff:
```python
import functools
import math

import jax
import jax.numpy as jnp
import ml_dtypes
import numpy as np
from jax import lax
from jax.experimental import pallas as pl
from jax.experimental.pallas import tpu as pltpu
from jax.sharding import PartitionSpec as P

MESH = pl.DeviceIdType.MESH
F32 = jnp.float32
BF16 = jnp.bfloat16

NF = 256
TOTAL = 131072
TBLK = 8192
OWN = 256
BLK = 128
PATCHES = 16
N_TM = 16
N_SPIN = 32
NY = 8
ROWS = 80
OUT_ROWS = 24
CHIRP = 0.015625
FLOOR = 1e-6


def cos_coefficients():
    nodes = 0.125 * (1.0 + np.cos(np.pi * (np.arange(64) + 0.5) / 64))
    fit = np.polynomial.chebyshev.Chebyshev.fit(
        nodes, np.cos(2.0 * np.pi * np.sqrt(nodes)), 8, domain=[0.0, 0.25]
    )
    return [float(c) for c in fit.convert(kind=np.polynomial.Polynomial).coef]


COS = cos_coefficients()


def cos_turns(x):
    y = x - jnp.floor(x + 0.5)
    square = y * y
    value = jnp.full_like(square, COS[-1])
    for c in COS[-2::-1]:
        value = value * square + c
    return value


@functools.lru_cache(None)
def bin_table():
    tau = np.arange(TBLK, dtype=np.int64).reshape(2, NY, 2 * OWN)
    tau = tau.transpose(1, 0, 2).reshape(NY, 1, 4 * OWN)
    index = (tau * np.arange(NF)[None, :, None]) % TOTAL
    angles = np.float32(2.0 * math.pi) * index.astype(np.float32) / np.float32(TOTAL)
    angles = angles.astype(np.float64)
    table = np.concatenate([np.cos(angles), np.sin(angles)], axis=1)
    return table.astype(np.float32).astype(ml_dtypes.bfloat16)


def kernel(
    strain_in, start_in, frac_in, antenna_in, spin_ref, table_in, out_ref,
    strain, halo, start, frac, antenna, table, turns, pieces, demod, acc, sums, landed,
    in_sems, table_sems, halo_send, halo_recv, send, recv, sum_send, sum_recv,
):
    tm, spin = lax.axis_index("tm"), lax.axis_index("spin")
    zl, y, c = spin // 16, (spin // 2) % NY, spin % 2
    linear = tm * N_SPIN + spin
    n_all = N_TM * N_SPIN

    def along(offset):
        other = (linear + offset + n_all) % n_all
        return (other // N_SPIN, other % N_SPIN)

    def at_y(offset):
        return (tm, zl * 16 + ((y + offset + NY) % NY) * 2 + c)

    def at_tm(offset):
        return ((tm + offset + N_TM) % N_TM, spin)

    at_z = (tm, (1 - zl) * 16 + y * 2 + c)
    at_c = (tm, zl * 16 + y * 2 + (1 - c))

    loads = [
        pltpu.make_async_copy(strain_in, strain, in_sems.at[0]),
        pltpu.make_async_copy(start_in, start, in_sems.at[1]),
        pltpu.make_async_copy(frac_in, frac, in_sems.at[2]),
        pltpu.make_async_copy(antenna_in, antenna, in_sems.at[3]),
    ]
    for load in loads:
        load.start()

    barrier = pltpu.get_barrier_semaphore()
    greeted = [along(1), along(-1), at_y(1), at_y(-1), at_y(2), at_y(-2), at_z, at_c]
    greeted += [at_tm(r) for r in range(1, N_TM)]
    for device in greeted:
        pl.semaphore_signal(barrier, inc=1, device_id=device, device_id_type=MESH)

    offsets = (0, -1, 1, -2, 2, -3, 3, 4)
    order = [(y + o + NY) % NY for o in offsets]
    table_loads = []
    for i, group in enumerate(order):
        load = pltpu.make_async_copy(table_in.at[group], table.at[group], table_sems.at[i])
        load.start()
        table_loads.append(load)

    for load in loads:
        load.wait()

    pl.semaphore_wait(barrier, len(greeted))

    halos = []
    for i, offset in enumerate((1, -1)):
        source = strain.at[:, pl.ds(BLK, BLK)] if offset == 1 else strain.at[:, pl.ds(0, BLK)]
        copy = pltpu.make_async_remote_copy(
            src_ref=source, dst_ref=halo.at[i], send_sem=halo_send.at[i], recv_sem=halo_recv.at[i],
            device_id=along(offset), device_id_type=MESH,
        )
        copy.start()
        halos.append(copy)

    row = lax.broadcasted_iota(jnp.int32, (8, 4 * OWN), 0)
    lane = lax.broadcasted_iota(jnp.int32, (8, 4 * OWN), 1)
    trial = row % 4
    index = jnp.where(trial == 0, spin_ref[0], jnp.where(trial == 1, spin_ref[1], jnp.where(trial == 2, spin_ref[2], spin_ref[3])))
    rate = index.astype(F32) * CHIRP
    quarter = jnp.where(row < 4, 0.0, 0.25)
    first = tm * TBLK + (lane // (2 * OWN)) * (TBLK // 2) + lane % (2 * OWN)

    def one_turn(group, carry):
        scaled = (first + group * (2 * OWN)).astype(F32) / TOTAL
        cycles = rate * (scaled * scaled)
        turns[group] = cos_turns((cycles - jnp.floor(cycles)) - quarter)
        return carry

    lax.fori_loop(0, NY, one_turn, 0)

    patterns = [[antenna[k, :, d, :] for d in range(2)] for k in range(2)]
    squares = []
    for k in range(2):
        square = patterns[k][0] * patterns[k][0] + patterns[k][1] * patterns[k][1]
        squares.append(square[:, :BLK] + square[:, BLK:])
    column = jnp.concatenate(squares * 4, axis=0)
    norm = jnp.sum(column.T, axis=0, keepdims=True)
    high = norm.astype(BF16).astype(F32)
    middle = (norm - high).astype(BF16).astype(F32)
    low = norm - high - middle
    row16 = lax.broadcasted_iota(jnp.int32, (16, BLK), 0)
    carried = jnp.where(row16 == 0, high, jnp.where(row16 == 1, middle, jnp.where(row16 == 2, low, 0.0)))
    own = pieces.at[y, zl * 2 + c]
    own[64:80, 0:BLK] = carried.astype(BF16)
    own[64:80, BLK:] = jnp.zeros((16, BLK), BF16)

    block_lane = lax.broadcasted_iota(jnp.int32, (PATCHES, 64), 1)
    lane128 = lax.broadcasted_iota(jnp.int32, (PATCHES, BLK), 1)
    places, weights = [], []
    for block in range(2):
        mine = block_lane == spin * 2 + block
        shift = jnp.sum(jnp.where(mine, start[...].astype(F32), 0.0), axis=1, keepdims=True)
        u = jnp.sum(jnp.where(mine, frac[...], 0.0), axis=1, keepdims=True)
        places.append(lane128 + (BLK - 1) + shift.astype(jnp.int32))
        up, low1, low2 = u + 1.0, u - 1.0, u - 2.0
        taps = (-u * low1 * low2 / 6.0, up * low1 * low2 / 2.0, -up * u * low2 / 2.0, up * u * low1 / 6.0)
        weights.append([jnp.broadcast_to(w, (PATCHES, BLK)) for w in taps])

    for copy in halos:
        copy.wait()
    before = jnp.where(linear == 0, 0.0, halo[0])
    after = jnp.where(linear == n_all - 1, 0.0, halo[1])
    tiles = [before, strain[:, :BLK], strain[:, BLK:], after]

    for block in range(2):
        resampled = []
        for r in range(4):
            wide = [jnp.broadcast_to(tiles[block + i][r : r + 1], (PATCHES, BLK)) for i in range(3)]
            total = None
            for m in range(4):
                place = places[block] + m
                within = place & (BLK - 1)
                got = [jnp.take_along_axis(t, within, axis=1) for t in wide]
                tap = jnp.where(place < BLK, got[0], jnp.where(place < 2 * BLK, got[1], got[2]))
                term = weights[block][m] * tap
                total = term if total is None else total + term
            resampled.append(total)
        lanes = slice(block * BLK, (block + 1) * BLK)
        for part in range(2):
            for k in range(2):
                value = patterns[k][0][:, lanes] * resampled[part] + patterns[k][1][:, lanes] * resampled[2 + part]
                own[part * 32 + k * 16 : part * 32 + k * 16 + 16, lanes] = value.astype(BF16)

    started = []

    def put(offset, z, core, device):
        i = len(started)
        at = pieces.at[(y + offset + NY) % NY, (zl if z == 0 else 1 - zl) * 2 + (c if core == 0 else 1 - c)]
        copy = pltpu.make_async_remote_copy(
            src_ref=at, dst_ref=at, send_sem=send.at[i], recv_sem=recv.at[i], device_id=device, device_id_type=MESH,
        )
        copy.start()
        started.append(copy)
        return copy

    along_y, along_z, along_c = {}, {}, {}

    def pass_on(offset, z):
        along_c[offset, z] = put(offset, z, 0, at_c)

    along_y[-1] = put(0, 0, 0, at_y(1))
    along_y[1] = put(0, 0, 0, at_y(-1))
    along_y[-2] = put(0, 0, 0, at_y(2))
    along_y[2] = put(0, 0, 0, at_y(-2))
    along_z[0] = put(0, 0, 0, at_z)
    pass_on(0, 0)

    def landed_y(offset):
        along_y[offset].wait_recv()
        if offset == -2:
            along_y[-3] = put(-2, 0, 0, at_y(1))
            along_y[4] = put(-2, 0, 0, at_y(2))
        if offset == 2:
            along_y[3] = put(2, 0, 0, at_y(-1))
        along_z[offset] = put(offset, 0, 0, at_z)
        pass_on(offset, 0)

    def landed_z(offset):
        along_z[offset].wait_recv()
        pass_on(offset, 1)

    def multiply(i):
        offset = offsets[i]
        along_c[offset, 0].wait_recv()
        along_c[offset, 1].wait_recv()
        group = order[i]
        table_loads[i].wait()
        held = demod.at[i % 2]
        for q in range(4):
            lanes = slice(q * OWN, (q + 1) * OWN)
            u = pieces[group, q, 0:32, :].astype(F32)
            v = pieces[group, q, 32:64, :].astype(F32)
            for s in range(4):
                cosine = turns[group, s : s + 1, lanes]
                sine = turns[group, 4 + s : 5 + s, lanes]
                held[s * 32 : s * 32 + 32, lanes] = (u * cosine + v * sine).astype(BF16)
                held[128 + s * 32 : 160 + s * 32, lanes] = (v * cosine - u * sine).astype(BF16)
        product = lax.dot_general(
            table[group], held[...], (((1,), (1,)), ((), ())), preferred_element_type=F32
        )
        acc[...] = product if i == 0 else acc[...] + product

    landed_y(-1)
    landed_y(1)
    landed_z(0)
    landed_y(-2)
    landed_y(2)
    multiply(0)
    landed_z(-1)
    landed_z(1)
    landed_y(-3)
    landed_y(3)
    multiply(1)
    landed_y(4)
    landed_z(-2)
    landed_z(2)
    multiply(2)
    landed_z(-3)
    landed_z(3)
    landed_z(4)
    for i in range(3, NY):
        multiply(i)

    def add_norms(j, total):
        return total + pieces[j // 4, j % 4, 64:80, 0:BLK].astype(F32)

    block_norm = lax.fori_loop(0, N_SPIN, add_norms, jnp.zeros((16, BLK), F32))
    block_norm = jnp.broadcast_to(jnp.sum(block_norm, axis=0, keepdims=True), (8, BLK))

    step = (lax.broadcasted_iota(jnp.int32, (16, BLK), 0) * tm) % 16
    turn = step.astype(F32) / 16.0
    cosine, sine = cos_turns(turn), cos_turns(turn - 0.25)

    def spectrum(to):
        low_row = pl.multiple_of(to * 16, 16)
        with_cos = acc[pl.ds(low_row, 16), :]
        with_sin = acc[pl.ds(low_row + NF, 16), :]
        real = with_cos[:, :BLK] + with_sin[:, BLK:]
        imag = with_cos[:, BLK:] - with_sin[:, :BLK]
        sums[to, 0:16, 0:BLK] = real * cosine + imag * sine
        sums[to, 0:16, BLK:] = imag * cosine - real * sine
        sums[to, 16:24, 0:BLK] = block_norm
        sums[to, 16:24, BLK:] = block_norm

    copies = []
    for r in range(1, N_TM):
        to = (tm + r) % N_TM
        spectrum(to)
        copy = pltpu.make_async_remote_copy(
            src_ref=sums.at[to], dst_ref=landed.at[r - 1], send_sem=sum_send.at[r - 1], recv_sem=sum_recv.at[r - 1],
            device_id=at_tm(r), device_id_type=MESH,
        )
        copy.start()
        copies.append(copy)
    spectrum(tm)
    for copy in started:
        copy.wait_send()
    total = sums[tm]
    for r, copy in enumerate(copies):
        copy.wait_recv()
        total = total + landed[r]
    inverse = 1.0 / (total[16:17, 0:BLK] + FLOOR)
    real, imag = total[0:16, 0:BLK], total[0:16, BLK:]
    power = (real * real + imag * imag) * inverse
    power = jnp.concatenate([power] * 8, axis=0).T
    for s in range(4):
        out_ref[s] = power[s * 32 : s * 32 + 16, 0:16] + power[s * 32 + 16 : s * 32 + 32, 0:16]
    for copy in copies:
        copy.wait_send()


def body(strain, stencil_start, stencil_frac, antenna, spin_index):
    table = jnp.asarray(bin_table())
    anywhere = pl.BlockSpec(memory_space=pl.ANY)
    dma = pltpu.SemaphoreType.DMA
    return pl.pallas_call(
        kernel,
        out_shape=jax.ShapeDtypeStruct((4, PATCHES, NF // N_TM), F32),
        in_specs=[anywhere] * 4 + [pl.BlockSpec(memory_space=pltpu.SMEM), anywhere],
        out_specs=pl.BlockSpec(memory_space=pltpu.VMEM),
        scratch_shapes=[
            pltpu.VMEM((4, OWN), F32),
            pltpu.VMEM((2, 4, BLK), F32),
            pltpu.VMEM((PATCHES, 64), jnp.int32),
            pltpu.VMEM((PATCHES, 64), F32),
            pltpu.VMEM((2, PATCHES, 2, OWN), F32),
            pltpu.VMEM((NY, 2 * NF, 4 * OWN), BF16),
            pltpu.VMEM((NY, 8, 4 * OWN), F32),
            pltpu.VMEM((NY, 4, ROWS, OWN), BF16),
            pltpu.VMEM((2, 256, 4 * OWN), BF16),
            pltpu.VMEM((2 * NF, 256), F32),
            pltpu.VMEM((N_TM, OUT_ROWS, 256), F32),
            pltpu.VMEM((N_TM - 1, OUT_ROWS, 256), F32),
            dma((4,)), dma((NY,)), dma((2,)), dma((2,)), dma((31,)), dma((31,)), dma((15,)), dma((15,)),
        ],
        compiler_params=pltpu.CompilerParams(
            collective_id=0, has_side_effects=True, vmem_limit_bytes=40 * 2**20
        ),
        name="search",
    )(strain, stencil_start, stencil_frac, antenna, spin_index, table)


def solution(mesh):
    return jax.shard_map(
        body,
        mesh=mesh,
        in_specs=(
            P(None, ("tm", "spin")),
            P(None, "tm"),
            P(None, "tm"),
            P(None, None, None, ("tm", "spin")),
            P("spin"),
        ),
        out_specs=P("spin", None, "tm"),
        check_vma=False,
    )
```

time: 407 us -> 55.4 us (0.14)
  the two profiles are of different devices: /device:TPU:24 before, /device:TPU:14 now
where the time goes in v1:
time: 55.4 us; the launch traced here: 55.1 us
  Pallas kernels  47.5 us (86%)
  local copies, waits for them, and re-layouts  7.57 us (14%)
    pallas_call x1, Pallas kernels, body(): pl.pallas_call(kernel, out_shape=jax.ShapeDtypeStruct((4, PATCHES, NF //...  47.5 us
    unnamed x13, local copies, waits for them, and re-layouts  7.57 us

profile of v1, /device:TPU:14, one launch (start us, length us, event | category | flops | bytes accessed | tf_op | source)
XLA Modules:
  0.0 55.1 jit_solution(5296137032697277213)
XLA Ops:
  0.0 0.0 copy-start
  0.0 3.4 %copy-done = bf16[8,512,1024]{2,1,0:T(8,128)(2,1)S(1)} copy-done((bf16[8,512,1024]{2,1,0:T(8,128)(2,1)S(1)}, bf16[8,512,1024]{2,1,0:T(8,128)(2,1)}, u32[]{:S(2)}) %copy-start) | copy-done | bytes 8388632
  3.4 0.0 copy-start.1
  3.4 0.8 %copy-done.1 = f32[2,16,2,256]{3,2,1,0:T(2,128)S(1)} copy-done((f32[2,16,2,256]{3,2,1,0:T(2,128)S(1)}, f32[2,16,2,256]{3,2,1,0:T(2,128)}, u32[]{:S(2)}) %copy-start.1) | copy-done | bytes 65560
  4.2 0.0 copy-start.2
  4.2 0.7 %copy-done.2 = s32[16,64]{1,0:T(8,128)S(1)} copy-done((s32[16,64]{1,0:T(8,128)S(1)}, s32[16,64]{1,0:T(8,128)}, u32[]{:S(2)}) %copy-start.2) | copy-done | bytes 4120
  4.9 0.0 copy-start.3
  4.9 0.7 %copy-done.3 = f32[16,64]{1,0:T(8,128)S(1)} copy-done((f32[16,64]{1,0:T(8,128)S(1)}, f32[16,64]{1,0:T(8,128)}, u32[]{:S(2)}) %copy-start.3) | copy-done | bytes 4120
  5.6 0.0 copy-start.4
  5.6 0.7 %copy-done.4 = f32[4,256]{1,0:T(4,128)S(1)} copy-done((f32[4,256]{1,0:T(4,128)S(1)}, f32[4,256]{1,0:T(4,128)}, u32[]{:S(2)}) %copy-start.4) | copy-done | bytes 4120
  6.3 0.0 copy-start.5
  6.3 0.7 %copy-done.5 = s32[4]{0:T(128)S(1)} copy-done((s32[4]{0:T(128)S(1)}, s32[4]{0:T(128)}, u32[]{:S(2)}) %copy-start.5) | copy-done | bytes 40
  7.0 47.5 %search.1 = f32[4,16,16]{2,1,0:T(8,128)S(1)} custom-call(f32[4,256]{1,0:T(4,128)S(1)} %copy-done.4, s32[16,64]{1,0:T(8,128)S(1)} %copy-done.2, f32[16,64]{1,0:T(8,128)S(1)} %copy-done.3, f32[2,16,2,256]{3,2,1,0:T(2,128)S(1)} %copy-done.1, s32[4]{0:T(128)S(1)} %copy-done.5, bf16[8,512,1024]{2,1,0:T(8,128)(2,1)S(1)} %copy-done), custom_call_target="tpu_custom_call" | custom-call | tf_op jit(solution)/shard_map/search/pallas_call | solution.py:325
  54.4 0.6 %copy.8 = f32[4,16,16]{2,1,0:T(8,128)} copy(f32[4,16,16]{2,1,0:T(8,128)S(1)} %search.1) | data formatting | bytes 8192
Async XLA Ops:
  0.0 3.4 %copy-start = (bf16[8,512,1024]{2,1,0:T(8,128)(2,1)S(1)}, bf16[8,512,1024]{2,1,0:T(8,128)(2,1)}, u32[]{:S(2)}) copy-start(bf16[8,512,1024]{2,1,0:T(8,128)(2,1)} %constant.2.clone.table_in) | copy-start | bytes 25165828
  3.4 0.8 %copy-start.1 = (f32[2,16,2,256]{3,2,1,0:T(2,128)S(1)}, f32[2,16,2,256]{3,2,1,0:T(2,128)}, u32[]{:S(2)}) copy-start(f32[2,16,2,256]{3,2,1,0:T(2,128)} %antenna_in.1) | copy-start | bytes 196612
  4.2 0.7 %copy-start.2 = (s32[16,64]{1,0:T(8,128)S(1)}, s32[16,64]{1,0:T(8,128)}, u32[]{:S(2)}) copy-start(s32[16,64]{1,0:T(8,128)} %start_in.1) | copy-start | bytes 12292
  4.9 0.7 %copy-start.3 = (f32[16,64]{1,0:T(8,128)S(1)}, f32[16,64]{1,0:T(8,128)}, u32[]{:S(2)}) copy-start(f32[16,64]{1,0:T(8,128)} %frac_in.1) | copy-start | bytes 12292
  5.6 0.7 %copy-start.4 = (f32[4,256]{1,0:T(4,128)S(1)}, f32[4,256]{1,0:T(4,128)}, u32[]{:S(2)}) copy-start(f32[4,256]{1,0:T(4,128)} %strain_in.1) | copy-start | bytes 12292
  6.3 0.7 %copy-start.5 = (s32[4]{0:T(128)S(1)}, s32[4]{0:T(128)}, u32[]{:S(2)}) copy-start(s32[4]{0:T(128)} %spin_ref.1) | copy-start | bytes 52

commit v2 on v1

--- a/solution.py
+++ b/solution.py
@@ -23,8 +23,9 @@
 N_TM = 16
 N_SPIN = 32
 NY = 8
-ROWS = 80
-OUT_ROWS = 24
+NX = 4
+NZ = 4
+ROWS = 64
 CHIRP = 0.015625
 FLOOR = 1e-6
 
@@ -62,11 +63,12 @@
 
 def kernel(
     strain_in, start_in, frac_in, antenna_in, spin_ref, table_in, out_ref,
-    strain, halo, start, frac, antenna, table, turns, pieces, demod, acc, sums, landed,
-    in_sems, table_sems, halo_send, halo_recv, send, recv, sum_send, sum_recv,
+    strain, halo, start, frac, antenna, table, turns, pieces, demod, acc, sums, landed_x, sent_z, landed_z_sum, norms, norms_in,
+    in_sems, table_sems, halo_send, halo_recv, send, recv, x_send, x_recv, z_send, z_recv, norm_send, norm_recv,
 ):
     tm, spin = lax.axis_index("tm"), lax.axis_index("spin")
     zl, y, c = spin // 16, (spin // 2) % NY, spin % 2
+    zh, x = tm // NX, tm % NX
     linear = tm * N_SPIN + spin
     n_all = N_TM * N_SPIN
 
@@ -77,8 +79,11 @@
     def at_y(offset):
         return (tm, zl * 16 + ((y + offset + NY) % NY) * 2 + c)
 
-    def at_tm(offset):
-        return ((tm + offset + N_TM) % N_TM, spin)
+    def at_x(offset):
+        return (zh * NX + (x + offset) % NX, spin)
+
+    def at_zh(offset):
+        return (((zh + offset) % NZ) * NX + x, spin)
 
     at_z = (tm, (1 - zl) * 16 + y * 2 + c)
     at_c = (tm, zl * 16 + y * 2 + (1 - c))
@@ -93,8 +98,8 @@
         load.start()
 
     barrier = pltpu.get_barrier_semaphore()
-    greeted = [along(1), along(-1), at_y(1), at_y(-1), at_y(2), at_y(-2), at_z, at_c]
-    greeted += [at_tm(r) for r in range(1, N_TM)]
+    greeted = [along(1), along(-1), at_z, at_c]
+    greeted += [at_y(r) for r in range(1, NY)] + [at_x(r) for r in range(1, NX)] + [at_zh(r) for r in range(1, NZ)]
     for device in greeted:
         pl.semaphore_signal(barrier, inc=1, device_id=device, device_id_type=MESH)
 
@@ -144,14 +149,32 @@
         squares.append(square[:, :BLK] + square[:, BLK:])
     column = jnp.concatenate(squares * 4, axis=0)
     norm = jnp.sum(column.T, axis=0, keepdims=True)
-    high = norm.astype(BF16).astype(F32)
-    middle = (norm - high).astype(BF16).astype(F32)
-    low = norm - high - middle
-    row16 = lax.broadcasted_iota(jnp.int32, (16, BLK), 0)
-    carried = jnp.where(row16 == 0, high, jnp.where(row16 == 1, middle, jnp.where(row16 == 2, low, 0.0)))
     own = pieces.at[y, zl * 2 + c]
-    own[64:80, 0:BLK] = carried.astype(BF16)
-    own[64:80, BLK:] = jnp.zeros((16, BLK), BF16)
+
+    norm_copies = []
+
+    def send_norms(step, devices):
+        copies = []
+        for device in devices:
+            i = len(norm_copies)
+            copy = pltpu.make_async_remote_copy(
+                src_ref=norms.at[step], dst_ref=norms_in.at[i], send_sem=norm_send.at[i], recv_sem=norm_recv.at[i],
+                device_id=device, device_id_type=MESH,
+            )
+            copy.start()
+            norm_copies.append(copy)
+            copies.append((i, copy))
+        return copies
+
+    def add_norms(step, copies):
+        total = norms[step]
+        for i, copy in copies:
+            copy.wait_recv()
+            total = total + norms_in[i]
+        norms[step + 1] = total
+
+    norms[0] = jnp.broadcast_to(norm, (8, BLK))
+    norms_c = send_norms(0, [at_c])
 
     block_lane = lax.broadcasted_iota(jnp.int32, (PATCHES, 64), 1)
     lane128 = lax.broadcasted_iota(jnp.int32, (PATCHES, BLK), 1)
@@ -192,9 +215,11 @@
 
     started = []
 
-    def put(offset, z, core, device):
+    def put(offset, z, device, rows=slice(None)):
         i = len(started)
-        at = pieces.at[(y + offset + NY) % NY, (zl if z == 0 else 1 - zl) * 2 + (c if core == 0 else 1 - c)]
+        at = pieces.at[(y + offset + NY) % NY, (zl if z == 0 else 1 - zl) * 2 + c]
+        if rows != slice(None):
+            at = at.at[pl.ds(rows.start, rows.stop - rows.start)]
         copy = pltpu.make_async_remote_copy(
             src_ref=at, dst_ref=at, send_sem=send.at[i], recv_sem=recv.at[i], device_id=device, device_id_type=MESH,
         )
@@ -203,30 +228,32 @@
         return copy
 
     along_y, along_z, along_c = {}, {}, {}
-
-    def pass_on(offset, z):
-        along_c[offset, z] = put(offset, z, 0, at_c)
-
-    along_y[-1] = put(0, 0, 0, at_y(1))
-    along_y[1] = put(0, 0, 0, at_y(-1))
-    along_y[-2] = put(0, 0, 0, at_y(2))
-    along_y[2] = put(0, 0, 0, at_y(-2))
-    along_z[0] = put(0, 0, 0, at_z)
-    pass_on(0, 0)
+    halves = (slice(0, 32), slice(32, 64))
+
+    along_y[-1] = [put(0, 0, at_y(1))]
+    along_y[1] = [put(0, 0, at_y(-1))]
+    along_z[0] = put(0, 0, at_z)
+    along_c[0, 0] = put(0, 0, at_c)
+    add_norms(0, norms_c)
+    norms_z = send_norms(1, [at_z])
 
     def landed_y(offset):
-        along_y[offset].wait_recv()
-        if offset == -2:
-            along_y[-3] = put(-2, 0, 0, at_y(1))
-            along_y[4] = put(-2, 0, 0, at_y(2))
-        if offset == 2:
-            along_y[3] = put(2, 0, 0, at_y(-1))
-        along_z[offset] = put(offset, 0, 0, at_z)
-        pass_on(offset, 0)
+        for copy in along_y[offset]:
+            copy.wait_recv()
+        if offset in (-1, -2):
+            along_y[offset - 1] = [put(offset, 0, at_y(1))]
+        if offset in (1, 2):
+            along_y[offset + 1] = [put(offset, 0, at_y(-1))]
+        if offset == -3:
+            along_y[4] = [put(-3, 0, at_y(1), halves[0])]
+        if offset == 3:
+            along_y[4].append(put(3, 0, at_y(-1), halves[1]))
+        along_z[offset] = put(offset, 0, at_z)
+        along_c[offset, 0] = put(offset, 0, at_c)
 
     def landed_z(offset):
         along_z[offset].wait_recv()
-        pass_on(offset, 1)
+        along_c[offset, 1] = put(offset, 1, at_c)
 
     def multiply(i):
         offset = offsets[i]
@@ -252,29 +279,32 @@
     landed_y(-1)
     landed_y(1)
     landed_z(0)
+    add_norms(1, norms_z)
+    norms_x = send_norms(2, [at_x(r) for r in range(1, NX)])
+    multiply(0)
     landed_y(-2)
     landed_y(2)
-    multiply(0)
     landed_z(-1)
     landed_z(1)
+    add_norms(2, norms_x)
+    norms_zh = send_norms(3, [at_zh(r) for r in range(1, NZ)])
+    multiply(1)
+    multiply(2)
     landed_y(-3)
     landed_y(3)
-    multiply(1)
-    landed_y(4)
     landed_z(-2)
     landed_z(2)
-    multiply(2)
+    add_norms(3, norms_zh)
+    norms_y = send_norms(4, [at_y(r) for r in range(1, NY)])
+    multiply(3)
+    multiply(4)
+    landed_y(4)
     landed_z(-3)
     landed_z(3)
+    multiply(5)
+    multiply(6)
     landed_z(4)
-    for i in range(3, NY):
-        multiply(i)
-
-    def add_norms(j, total):
-        return total + pieces[j // 4, j % 4, 64:80, 0:BLK].astype(F32)
-
-    block_norm = lax.fori_loop(0, N_SPIN, add_norms, jnp.zeros((16, BLK), F32))
-    block_norm = jnp.broadcast_to(jnp.sum(block_norm, axis=0, keepdims=True), (8, BLK))
+    multiply(7)
 
     step = (lax.broadcasted_iota(jnp.int32, (16, BLK), 0) * tm) % 16
     turn = step.astype(F32) / 16.0
@@ -286,41 +316,56 @@
         with_sin = acc[pl.ds(low_row + NF, 16), :]
         real = with_cos[:, :BLK] + with_sin[:, BLK:]
         imag = with_cos[:, BLK:] - with_sin[:, :BLK]
-        sums[to, 0:16, 0:BLK] = real * cosine + imag * sine
-        sums[to, 0:16, BLK:] = imag * cosine - real * sine
-        sums[to, 16:24, 0:BLK] = block_norm
-        sums[to, 16:24, BLK:] = block_norm
-
-    copies = []
-    for r in range(1, N_TM):
-        to = (tm + r) % N_TM
-        spectrum(to)
+        sums[to, :, 0:BLK] = real * cosine + imag * sine
+        sums[to, :, BLK:] = imag * cosine - real * sine
+
+    def step_copy(source, target, send_sem, recv_sem, device):
         copy = pltpu.make_async_remote_copy(
-            src_ref=sums.at[to], dst_ref=landed.at[r - 1], send_sem=sum_send.at[r - 1], recv_sem=sum_recv.at[r - 1],
-            device_id=at_tm(r), device_id_type=MESH,
+            src_ref=source, dst_ref=target, send_sem=send_sem, recv_sem=recv_sem, device_id=device, device_id_type=MESH,
         )
         copy.start()
-        copies.append(copy)
-    spectrum(tm)
+        return copy
+
+    z_offsets = (2, 1, 3, 0)
+    copies_x, copies_z = [], []
+    for q, dz in enumerate(z_offsets):
+        base = ((zh + dz) % NZ) * NX
+        group = []
+        for r in (2, 1, 3):
+            to = base + (x + r) % NX
+            spectrum(to)
+            i = q * 3 + r - 1
+            group.append(step_copy(sums.at[to], landed_x.at[i], x_send.at[i], x_recv.at[i], at_x(r)))
+        spectrum(base + x)
+        copies_x.append(group)
     for copy in started:
         copy.wait_send()
-    total = sums[tm]
-    for r, copy in enumerate(copies):
-        copy.wait_recv()
-        total = total + landed[r]
-    inverse = 1.0 / (total[16:17, 0:BLK] + FLOOR)
-    real, imag = total[0:16, 0:BLK], total[0:16, BLK:]
+    add_norms(4, norms_y)
+    for q, dz in enumerate(z_offsets):
+        total = sums[((zh + dz) % NZ) * NX + x]
+        for copy in copies_x[q]:
+            copy.wait_recv()
+        for r in range(3):
+            total = total + landed_x[q * 3 + r]
+        if dz:
+            sent_z[q] = total
+            copies_z.append(step_copy(sent_z.at[q], landed_z_sum.at[q], z_send.at[q], z_recv.at[q], at_zh(dz)))
+    for q in range(3):
+        copies_z[q].wait_recv()
+        total = total + landed_z_sum[q]
+    inverse = 1.0 / (norms[5, 0:1] + FLOOR)
+    real, imag = total[:, 0:BLK], total[:, BLK:]
     power = (real * real + imag * imag) * inverse
     power = jnp.concatenate([power] * 8, axis=0).T
     for s in range(4):
         out_ref[s] = power[s * 32 : s * 32 + 16, 0:16] + power[s * 32 + 16 : s * 32 + 32, 0:16]
-    for copy in copies:
+    for copy in sum(copies_x, []) + copies_z + norm_copies:
         copy.wait_send()
 
 
 def body(strain, stencil_start, stencil_frac, antenna, spin_index):
     table = jnp.asarray(bin_table())
-    anywhere = pl.BlockSpec(memory_space=pl.ANY)
+    anywhere = pl.BlockSpec(memory_space=pltpu.HBM)
     dma = pltpu.SemaphoreType.DMA
     return pl.pallas_call(
         kernel,
@@ -338,9 +383,14 @@
             pltpu.VMEM((NY, 4, ROWS, OWN), BF16),
             pltpu.VMEM((2, 256, 4 * OWN), BF16),
             pltpu.VMEM((2 * NF, 256), F32),
-            pltpu.VMEM((N_TM, OUT_ROWS, 256), F32),
-            pltpu.VMEM((N_TM - 1, OUT_ROWS, 256), F32),
-            dma((4,)), dma((NY,)), dma((2,)), dma((2,)), dma((31,)), dma((31,)), dma((15,)), dma((15,)),
+            pltpu.VMEM((N_TM, 16, 256), F32),
+            pltpu.VMEM((12, 16, 256), F32),
+            pltpu.VMEM((3, 16, 256), F32),
+            pltpu.VMEM((3, 16, 256), F32),
+            pltpu.VMEM((6, 8, BLK), F32),
+            pltpu.VMEM((15, 8, BLK), F32),
+            dma((4,)), dma((NY,)), dma((2,)), dma((2,)), dma((32,)), dma((32,)),
+            dma((12,)), dma((12,)), dma((3,)), dma((3,)), dma((15,)), dma((15,)),
         ],
         compiler_params=pltpu.CompilerParams(
             collective_id=0, has_side_effects=True, vmem_limit_bytes=40 * 2**20

time: 55.4 us -> 54.3 us (0.980)
  the two profiles are of different devices: /device:TPU:14 before, /device:TPU:1 now
where the time goes in v2:
time: 54.3 us; the launch traced here: 54 us
  Pallas kernels  46.4 us (85%)
  local copies, waits for them, and re-layouts  7.57 us (14%)
    pallas_call x1, Pallas kernels, body(): pl.pallas_call(kernel, out_shape=jax.ShapeDtypeStruct((4, PATCHES, NF //...  46.4 us
    unnamed x13, local copies, waits for them, and re-layouts  7.57 us

profile of v2, /device:TPU:1, one launch (start us, length us, event | category | flops | bytes accessed | tf_op | source)
XLA Modules:
  0.0 54.0 jit_solution(6280747727874813067)
XLA Ops:
  0.0 0.0 copy-start
  0.0 3.4 %copy-done = bf16[8,512,1024]{2,1,0:T(8,128)(2,1)S(1)} copy-done((bf16[8,512,1024]{2,1,0:T(8,128)(2,1)S(1)}, bf16[8,512,1024]{2,1,0:T(8,128)(2,1)}, u32[]{:S(2)}) %copy-start) | copy-done | bytes 8388632
  3.4 0.0 copy-start.1
  3.4 0.8 %copy-done.1 = f32[2,16,2,256]{3,2,1,0:T(2,128)S(1)} copy-done((f32[2,16,2,256]{3,2,1,0:T(2,128)S(1)}, f32[2,16,2,256]{3,2,1,0:T(2,128)}, u32[]{:S(2)}) %copy-start.1) | copy-done | bytes 65560
  4.2 0.0 copy-start.2
  4.2 0.7 %copy-done.2 = s32[16,64]{1,0:T(8,128)S(1)} copy-done((s32[16,64]{1,0:T(8,128)S(1)}, s32[16,64]{1,0:T(8,128)}, u32[]{:S(2)}) %copy-start.2) | copy-done | bytes 4120
  4.9 0.0 copy-start.3
  4.9 0.7 %copy-done.3 = f32[16,64]{1,0:T(8,128)S(1)} copy-done((f32[16,64]{1,0:T(8,128)S(1)}, f32[16,64]{1,0:T(8,128)}, u32[]{:S(2)}) %copy-start.3) | copy-done | bytes 4120
  5.6 0.0 copy-start.4
  5.6 0.7 %copy-done.4 = f32[4,256]{1,0:T(4,128)S(1)} copy-done((f32[4,256]{1,0:T(4,128)S(1)}, f32[4,256]{1,0:T(4,128)}, u32[]{:S(2)}) %copy-start.4) | copy-done | bytes 4120
  6.3 0.0 copy-start.5
  6.3 0.7 %copy-done.5 = s32[4]{0:T(128)S(1)} copy-done((s32[4]{0:T(128)S(1)}, s32[4]{0:T(128)}, u32[]{:S(2)}) %copy-start.5) | copy-done | bytes 40
  7.0 46.4 %search.1 = f32[4,16,16]{2,1,0:T(8,128)S(1)} custom-call(f32[4,256]{1,0:T(4,128)S(1)} %copy-done.4, s32[16,64]{1,0:T(8,128)S(1)} %copy-done.2, f32[16,64]{1,0:T(8,128)S(1)} %copy-done.3, f32[2,16,2,256]{3,2,1,0:T(2,128)S(1)} %copy-done.1, s32[4]{0:T(128)S(1)} %copy-done.5, bf16[8,512,1024]{2,1,0:T(8,128)(2,1)S(1)} %copy-done), custom_call_target="tpu_custom_call" | custom-call | tf_op jit(solution)/shard_map/search/pallas_call | solution.py:370
  53.4 0.6 %copy.8 = f32[4,16,16]{2,1,0:T(8,128)} copy(f32[4,16,16]{2,1,0:T(8,128)S(1)} %search.1) | data formatting | bytes 8192
Async XLA Ops:
  0.0 3.4 %copy-start = (bf16[8,512,1024]{2,1,0:T(8,128)(2,1)S(1)}, bf16[8,512,1024]{2,1,0:T(8,128)(2,1)}, u32[]{:S(2)}) copy-start(bf16[8,512,1024]{2,1,0:T(8,128)(2,1)} %constant.2.clone.table_in) | copy-start | bytes 25165828
  3.4 0.8 %copy-start.1 = (f32[2,16,2,256]{3,2,1,0:T(2,128)S(1)}, f32[2,16,2,256]{3,2,1,0:T(2,128)}, u32[]{:S(2)}) copy-start(f32[2,16,2,256]{3,2,1,0:T(2,128)} %antenna_in.1) | copy-start | bytes 196612
  4.2 0.7 %copy-start.2 = (s32[16,64]{1,0:T(8,128)S(1)}, s32[16,64]{1,0:T(8,128)}, u32[]{:S(2)}) copy-start(s32[16,64]{1,0:T(8,128)} %start_in.1) | copy-start | bytes 12292
  4.9 0.7 %copy-start.3 = (f32[16,64]{1,0:T(8,128)S(1)}, f32[16,64]{1,0:T(8,128)}, u32[]{:S(2)}) copy-start(f32[16,64]{1,0:T(8,128)} %frac_in.1) | copy-start | bytes 12292
  5.6 0.7 %copy-start.4 = (f32[4,256]{1,0:T(4,128)S(1)}, f32[4,256]{1,0:T(4,128)}, u32[]{:S(2)}) copy-start(f32[4,256]{1,0:T(4,128)} %strain_in.1) | copy-start | bytes 12292
  6.3 0.7 %copy-start.5 = (s32[4]{0:T(128)S(1)}, s32[4]{0:T(128)}, u32[]{:S(2)}) copy-start(s32[4]{0:T(128)} %spin_ref.1) | copy-start | bytes 52

commit v3 on v2

v3 whole, which is shorter than its diff:
```python
import functools
import math

import jax
import jax.numpy as jnp
import ml_dtypes
import numpy as np
from jax import lax
from jax.experimental import pallas as pl
from jax.experimental.pallas import tpu as pltpu
from jax.sharding import PartitionSpec as P

MESH = pl.DeviceIdType.MESH
F32 = jnp.float32
BF16 = jnp.bfloat16

NF = 256
TOTAL = 131072
TBLK = 8192
OWN = 256
BLK = 128
PATCHES = 16
N_TM = 16
N_SPIN = 32
NY = 8
NX = 4
NZ = 4
ROWS = 64
CHIRP = 0.015625
FLOOR = 1e-6


def cos_coefficients():
    nodes = 0.125 * (1.0 + np.cos(np.pi * (np.arange(64) + 0.5) / 64))
    fit = np.polynomial.chebyshev.Chebyshev.fit(
        nodes, np.cos(2.0 * np.pi * np.sqrt(nodes)), 8, domain=[0.0, 0.25]
    )
    return [float(c) for c in fit.convert(kind=np.polynomial.Polynomial).coef]


COS = cos_coefficients()


def cos_turns(x):
    y = x - jnp.floor(x + 0.5)
    square = y * y
    value = jnp.full_like(square, COS[-1])
    for c in COS[-2::-1]:
        value = value * square + c
    return value


@functools.lru_cache(None)
def bin_table():
    tau = np.arange(TBLK, dtype=np.int64).reshape(2, NY, 2 * OWN)
    tau = tau.transpose(1, 0, 2).reshape(2 * NY, 1, 2 * OWN)
    index = (tau * np.arange(NF)[None, :, None]) % TOTAL
    angles = np.float32(2.0 * math.pi) * index.astype(np.float32) / np.float32(TOTAL)
    angles = angles.astype(np.float64)
    table = np.concatenate([np.cos(angles), np.sin(angles)], axis=1)
    return table.astype(np.float32).astype(ml_dtypes.bfloat16)


def kernel(
    strain_in, start_in, frac_in, antenna_in, spin_ref, table_in, out_ref,
    strain, halo, start, frac, antenna, table, turns, pieces, demod, acc, sums, landed, norms, norms_in,
    in_sems, table_sems, halo_send, halo_recv, send, recv, sum_send, sum_recv, norm_send, norm_recv,
):
    tm, spin = lax.axis_index("tm"), lax.axis_index("spin")
    zl, y, c = spin // 16, (spin // 2) % NY, spin % 2
    zh, x = tm // NX, tm % NX
    linear = tm * N_SPIN + spin
    n_all = N_TM * N_SPIN

    def along(offset):
        other = (linear + offset + n_all) % n_all
        return (other // N_SPIN, other % N_SPIN)

    def at_y(offset, z=0):
        return (tm, (zl if z == 0 else 1 - zl) * 16 + ((y + offset + NY) % NY) * 2 + c)

    def tm_at(dz, dx):
        return ((zh + dz) % NZ) * NX + (x + dx) % NX

    at_z = at_y(0, 1)
    at_c = (tm, zl * 16 + y * 2 + (1 - c))

    loads = [
        pltpu.make_async_copy(strain_in, strain, in_sems.at[0]),
        pltpu.make_async_copy(start_in, start, in_sems.at[1]),
        pltpu.make_async_copy(frac_in, frac, in_sems.at[2]),
        pltpu.make_async_copy(antenna_in, antenna, in_sems.at[3]),
    ]
    for load in loads:
        load.start()

    barrier = pltpu.get_barrier_semaphore()
    shifts = [(dz, dx) for dz in (2, 1, 3, 0) for dx in (2, 1, 3, 0) if dz or dx]
    greeted = [(tm_at(dz, dx), spin) for dz, dx in shifts]
    greeted += [at_y(r) for r in range(1, NY)] + [at_y(r, 1) for r in (0, 1, -1, 2)]
    greeted += [along(1), along(-1), at_c]
    for device in greeted:
        pl.semaphore_signal(barrier, inc=1, device_id=device, device_id_type=MESH)

    offsets = (0, -1, 1, -2, 2, -3, 3, 4)
    order = [(y + o + NY) % NY for o in offsets]
    table_loads = []
    for i, group in enumerate(order):
        both = pl.ds(2 * group, 2)
        load = pltpu.make_async_copy(table_in.at[both], table.at[both], table_sems.at[i])
        load.start()
        table_loads.append(load)

    for load in loads:
        load.wait()

    pl.semaphore_wait(barrier, len(greeted))

    halos = []
    for i, offset in enumerate((1, -1)):
        source = strain.at[:, pl.ds(BLK, BLK)] if offset == 1 else strain.at[:, pl.ds(0, BLK)]
        copy = pltpu.make_async_remote_copy(
            src_ref=source, dst_ref=halo.at[i], send_sem=halo_send.at[i], recv_sem=halo_recv.at[i],
            device_id=along(offset), device_id_type=MESH,
        )
        copy.start()
        halos.append(copy)

    row = lax.broadcasted_iota(jnp.int32, (8, 2 * OWN), 0)
    lane = lax.broadcasted_iota(jnp.int32, (8, 2 * OWN), 1)
    trial = row % 4
    index = jnp.where(trial == 0, spin_ref[0], jnp.where(trial == 1, spin_ref[1], jnp.where(trial == 2, spin_ref[2], spin_ref[3])))
    rate = index.astype(F32) * CHIRP
    quarter = jnp.where(row < 4, 0.0, 0.25)
    first = tm * TBLK + lane

    def one_turn(group, carry):
        scaled = (first + (group % 2) * (TBLK // 2) + (group // 2) * (2 * OWN)).astype(F32) / TOTAL
        cycles = rate * (scaled * scaled)
        turns[group] = cos_turns((cycles - jnp.floor(cycles)) - quarter)
        return carry

    lax.fori_loop(0, 2 * NY, one_turn, 0)

    patterns = [[antenna[k, :, d, :] for d in range(2)] for k in range(2)]
    squares = []
    for k in range(2):
        square = patterns[k][0] * patterns[k][0] + patterns[k][1] * patterns[k][1]
        squares.append(square[:, :BLK] + square[:, BLK:])
    column = jnp.concatenate(squares * 4, axis=0)
    norm = jnp.sum(column.T, axis=0, keepdims=True)
    own = pieces.at[2 * y + zl, c]

    norm_copies = []

    def send_norms(step, devices):
        copies = []
        for device in devices:
            i = len(norm_copies)
            copy = pltpu.make_async_remote_copy(
                src_ref=norms.at[step], dst_ref=norms_in.at[i], send_sem=norm_send.at[i], recv_sem=norm_recv.at[i],
                device_id=device, device_id_type=MESH,
            )
            copy.start()
            norm_copies.append(copy)
            copies.append((i, copy))
        return copies

    def add_norms(step, copies):
        total = norms[step]
        for i, copy in copies:
            copy.wait_recv()
            total = total + norms_in[i]
        norms[step + 1] = total

    norms[0] = jnp.broadcast_to(norm, (8, BLK))
    norms_c = send_norms(0, [at_c])

    block_lane = lax.broadcasted_iota(jnp.int32, (PATCHES, 64), 1)
    lane128 = lax.broadcasted_iota(jnp.int32, (PATCHES, BLK), 1)
    places, weights = [], []
    for block in range(2):
        mine = block_lane == spin * 2 + block
        shift = jnp.sum(jnp.where(mine, start[...].astype(F32), 0.0), axis=1, keepdims=True)
        u = jnp.sum(jnp.where(mine, frac[...], 0.0), axis=1, keepdims=True)
        places.append(lane128 + (BLK - 1) + shift.astype(jnp.int32))
        up, low1, low2 = u + 1.0, u - 1.0, u - 2.0
        taps = (-u * low1 * low2 / 6.0, up * low1 * low2 / 2.0, -up * u * low2 / 2.0, up * u * low1 / 6.0)
        weights.append([jnp.broadcast_to(w, (PATCHES, BLK)) for w in taps])

    for copy in halos:
        copy.wait()
    before = jnp.where(linear == 0, 0.0, halo[0])
    after = jnp.where(linear == n_all - 1, 0.0, halo[1])
    tiles = [before, strain[:, :BLK], strain[:, BLK:], after]

    for block in range(2):
        resampled = []
        for r in range(4):
            wide = [jnp.broadcast_to(tiles[block + i][r : r + 1], (PATCHES, BLK)) for i in range(3)]
            total = None
            for m in range(4):
                place = places[block] + m
                within = place & (BLK - 1)
                got = [jnp.take_along_axis(t, within, axis=1) for t in wide]
                tap = jnp.where(place < BLK, got[0], jnp.where(place < 2 * BLK, got[1], got[2]))
                term = weights[block][m] * tap
                total = term if total is None else total + term
            resampled.append(total)
        lanes = slice(block * BLK, (block + 1) * BLK)
        for part in range(2):
            for k in range(2):
                value = patterns[k][0][:, lanes] * resampled[part] + patterns[k][1][:, lanes] * resampled[2 + part]
                own[part * 32 + k * 16 : part * 32 + k * 16 + 16, lanes] = value.astype(BF16)

    started = []

    def unit_of(offset, z):
        return 2 * ((y + offset + NY) % NY) + (zl if z == 0 else 1 - zl)

    def put(offset, z, device):
        i = len(started)
        at = pieces.at[unit_of(offset, z), c]
        copy = pltpu.make_async_remote_copy(
            src_ref=at, dst_ref=at, send_sem=send.at[i], recv_sem=recv.at[i], device_id=device, device_id_type=MESH,
        )
        copy.start()
        started.append(copy)
        return copy

    coming, sibling = {}, {}

    coming[2, 0] = put(0, 0, at_y(-2))
    coming[-2, 0] = put(0, 0, at_y(2))
    coming[1, 0] = put(0, 0, at_y(-1))
    coming[-1, 0] = put(0, 0, at_y(1))
    coming[0, 1] = put(0, 0, at_z)
    sibling[0, 0] = put(0, 0, at_c)
    add_norms(0, norms_c)
    norms_z = send_norms(1, [at_z])

    def landed_at(offset, z):
        coming[offset, z].wait_recv()
        if (offset, z) == (-2, 0):
            coming[4, 0] = put(-2, 0, at_y(2))
            coming[-3, 1] = put(-2, 0, at_y(1, 1))
            coming[-3, 0] = put(-2, 0, at_y(1))
        if (offset, z) == (2, 0):
            coming[4, 1] = put(2, 0, at_y(-2, 1))
            coming[3, 1] = put(2, 0, at_y(-1, 1))
            coming[3, 0] = put(2, 0, at_y(-1))
        if z == 0 and abs(offset) <= 2:
            coming[offset, 1] = put(offset, 0, at_z)
        sibling[offset, z] = put(offset, z, at_c)

    multiplied = []

    def multiply(offset, z):
        sibling[offset, z].wait_recv()
        if offset not in multiplied:
            table_loads[offsets.index(offset)].wait()
        unit = unit_of(offset, z)
        held = demod.at[len(multiplied) % 2]
        for q in range(2):
            lanes = slice(q * OWN, (q + 1) * OWN)
            u = pieces[unit, q, 0:32, :].astype(F32)
            v = pieces[unit, q, 32:64, :].astype(F32)
            for s in range(4):
                cosine = turns[unit, s : s + 1, lanes]
                sine = turns[unit, 4 + s : 5 + s, lanes]
                held[s * 32 : s * 32 + 32, lanes] = (u * cosine + v * sine).astype(BF16)
                held[128 + s * 32 : 160 + s * 32, lanes] = (v * cosine - u * sine).astype(BF16)
        product = lax.dot_general(
            table[unit], held[...], (((1,), (1,)), ((), ())), preferred_element_type=F32
        )
        acc[...] = acc[...] + product if multiplied else product
        multiplied.append(offset)

    for offset, z in ((-2, 0), (2, 0), (-1, 0), (1, 0), (0, 1)):
        landed_at(offset, z)
    add_norms(1, norms_z)
    norms_x = send_norms(2, [(tm_at(0, dx), spin) for dx in range(1, NX)])
    for offset, z in ((0, 0), (-2, 0), (2, 0), (-1, 0), (1, 0), (0, 1)):
        multiply(offset, z)
    waiting = []
    for pair in (((-2, 1), (2, 1)), ((-1, 1), (1, 1)), ((-3, 0), (3, 0)), ((-3, 1), (3, 1)), ((4, 0), (4, 1))):
        for offset, z in pair:
            landed_at(offset, z)
        if len(waiting) == 2:
            add_norms(2, norms_x)
            norms_zh = send_norms(3, [(tm_at(dz, 0), spin) for dz in range(1, NZ)])
        for offset, z in waiting[-1:] and waiting[-1]:
            multiply(offset, z)
        waiting.append(pair)
    for offset, z in waiting[-1]:
        multiply(offset, z)
    add_norms(3, norms_zh)
    norms_y = send_norms(4, [at_y(r) for r in range(1, NY)])

    step = (lax.broadcasted_iota(jnp.int32, (16, BLK), 0) * tm) % 16
    turn = step.astype(F32) / 16.0
    cosine, sine = cos_turns(turn), cos_turns(turn - 0.25)

    def spectrum(to):
        low_row = pl.multiple_of(to * 16, 16)
        with_cos = acc[pl.ds(low_row, 16), :]
        with_sin = acc[pl.ds(low_row + NF, 16), :]
        real = with_cos[:, :BLK] + with_sin[:, BLK:]
        imag = with_cos[:, BLK:] - with_sin[:, :BLK]
        sums[to, :, 0:BLK] = real * cosine + imag * sine
        sums[to, :, BLK:] = imag * cosine - real * sine

    copies = []
    for i, (dz, dx) in enumerate(shifts):
        to = tm_at(dz, dx)
        spectrum(to)
        copy = pltpu.make_async_remote_copy(
            src_ref=sums.at[to], dst_ref=landed.at[i], send_sem=sum_send.at[i], recv_sem=sum_recv.at[i],
            device_id=(to, spin), device_id_type=MESH,
        )
        copy.start()
        copies.append(copy)
    spectrum(tm)
    for copy in started:
        copy.wait_send()
    total = sums[tm]
    for i in reversed(range(len(copies))):
        copies[i].wait_recv()
        total = total + landed[i]
    add_norms(4, norms_y)
    inverse = 1.0 / (norms[5, 0:1] + FLOOR)
    real, imag = total[:, 0:BLK], total[:, BLK:]
    power = (real * real + imag * imag) * inverse
    power = jnp.concatenate([power] * 8, axis=0).T
    for s in range(4):
        out_ref[s] = power[s * 32 : s * 32 + 16, 0:16] + power[s * 32 + 16 : s * 32 + 32, 0:16]
    for copy in copies + norm_copies:
        copy.wait_send()


def body(strain, stencil_start, stencil_frac, antenna, spin_index):
    table = jnp.asarray(bin_table())
    anywhere = pl.BlockSpec(memory_space=pl.ANY)
    dma = pltpu.SemaphoreType.DMA
    return pl.pallas_call(
        kernel,
        out_shape=jax.ShapeDtypeStruct((4, PATCHES, NF // N_TM), F32),
        in_specs=[anywhere] * 4 + [pl.BlockSpec(memory_space=pltpu.SMEM), anywhere],
        out_specs=pl.BlockSpec(memory_space=pltpu.VMEM),
        scratch_shapes=[
            pltpu.VMEM((4, OWN), F32),
            pltpu.VMEM((2, 4, BLK), F32),
            pltpu.VMEM((PATCHES, 64), jnp.int32),
            pltpu.VMEM((PATCHES, 64), F32),
            pltpu.VMEM((2, PATCHES, 2, OWN), F32),
            pltpu.VMEM((2 * NY, 2 * NF, 2 * OWN), BF16),
            pltpu.VMEM((2 * NY, 8, 2 * OWN), F32),
            pltpu.VMEM((2 * NY, 2, ROWS, OWN), BF16),
            pltpu.VMEM((2, 256, 2 * OWN), BF16),
            pltpu.VMEM((2 * NF, 256), F32),
            pltpu.VMEM((N_TM, 16, 256), F32),
            pltpu.VMEM((N_TM - 1, 16, 256), F32),
            pltpu.VMEM((6, 8, BLK), F32),
            pltpu.VMEM((15, 8, BLK), F32),
            dma((4,)), dma((NY,)), dma((2,)), dma((2,)), dma((31,)), dma((31,)),
            dma((15,)), dma((15,)), dma((15,)), dma((15,)),
        ],
        compiler_params=pltpu.CompilerParams(
            collective_id=0, has_side_effects=True, vmem_limit_bytes=60 * 2**20
        ),
        name="search",
    )(strain, stencil_start, stencil_frac, antenna, spin_index, table)


def solution(mesh):
    return jax.shard_map(
        body,
        mesh=mesh,
        in_specs=(
            P(None, ("tm", "spin")),
            P(None, "tm"),
            P(None, "tm"),
            P(None, None, None, ("tm", "spin")),
            P("spin"),
        ),
        out_specs=P("spin", None, "tm"),
        check_vma=False,
    )
```

time: 54.3 us -> 46.3 us (0.85)
  local copies, waits for them, and re-layouts: 7.57 us -> 1.38 us
  Pallas kernels: 46.4 us -> 44.7 us
    unnamed x13 -> x1, local copies, waits for them, and re-layouts: 7.57 us -> 1.38 us
    pallas_call x1, Pallas kernels: 46.4 us -> 44.7 us  [body(): pl.pallas_call(kernel, out_shape=jax.ShapeDtypeStruct((4, PATCHES, NF //...]
where the time goes in v3:
time: 46.3 us; the launch traced here: 46.1 us
  Pallas kernels  44.7 us (97%)
  local copies, waits for them, and re-layouts  1.38 us (3%)
    pallas_call x1, Pallas kernels, body(): pl.pallas_call(kernel, out_shape=jax.ShapeDtypeStruct((4, PATCHES, NF //...  44.7 us
    unnamed x1, local copies, waits for them, and re-layouts  1.38 us

profile of v3, /device:TPU:1, one launch (start us, length us, event | category | flops | bytes accessed | tf_op | source)
XLA Modules:
  0.0 46.1 jit_solution(1750434793843580750)
XLA Ops:
  0.0 44.7 %search.1 = f32[4,16,16]{2,1,0:T(8,128)} custom-call(f32[4,256]{1,0:T(4,128)} %strain_in.1, s32[16,64]{1,0:T(8,128)} %start_in.1, f32[16,64]{1,0:T(8,128)} %frac_in.1, f32[2,16,2,256]{3,2,1,0:T(2,128)} %antenna_in.1, s32[4]{0:T(128)} %spin_ref.1, bf16[16,512,512]{2,1,0:T(8,128)(2,1)} %constant.2.clone.table_in), custom_call_target="tpu_custom_call" | custom-call | tf_op jit(solution)/shard_map/search/pallas_call | solution.py:345
  44.8 1.4 %copy.8 = f32[4,16,16]{2,1,0:T(8,128)} copy(f32[4,16,16]{2,1,0:T(8,128)} %search.1) | data formatting | bytes 8192

commit v4 on v3

--- a/solution.py
+++ b/solution.py
@@ -62,8 +62,8 @@
 
 
 def kernel(
-    strain_in, start_in, frac_in, antenna_in, spin_ref, table_in, out_ref,
-    strain, halo, start, frac, antenna, table, turns, pieces, demod, acc, sums, landed, norms, norms_in,
+    strain_in, start_in, frac_in, antenna_in, spin_in, table_in, out_ref,
+    strain, spin_ref, halo, start, frac, antenna, table, turns, pieces, demod, acc, sums, landed, norms, norms_in,
     in_sems, table_sems, halo_send, halo_recv, send, recv, sum_send, sum_recv, norm_send, norm_recv,
 ):
     tm, spin = lax.axis_index("tm"), lax.axis_index("spin")
@@ -90,15 +90,15 @@
         pltpu.make_async_copy(start_in, start, in_sems.at[1]),
         pltpu.make_async_copy(frac_in, frac, in_sems.at[2]),
         pltpu.make_async_copy(antenna_in, antenna, in_sems.at[3]),
+        pltpu.make_async_copy(spin_in, spin_ref, in_sems.at[4]),
     ]
     for load in loads:
         load.start()
 
     barrier = pltpu.get_barrier_semaphore()
     shifts = [(dz, dx) for dz in (2, 1, 3, 0) for dx in (2, 1, 3, 0) if dz or dx]
-    greeted = [(tm_at(dz, dx), spin) for dz, dx in shifts]
-    greeted += [at_y(r) for r in range(1, NY)] + [at_y(r, 1) for r in (0, 1, -1, 2)]
-    greeted += [along(1), along(-1), at_c]
+    greeted = [along(1), along(-1), at_c] + [at_y(r) for r in (1, -1, 2, -2)] + [at_y(r, 1) for r in (0, 1, -1, 2)]
+    greeted += [(tm_at(0, dx), spin) for dx in (1, 2, 3)] + [(tm_at(dz, 0), spin) for dz in (1, 3)]
     for device in greeted:
         pl.semaphore_signal(barrier, inc=1, device_id=device, device_id_type=MESH)
 
@@ -111,9 +111,7 @@
         load.start()
         table_loads.append(load)
 
-    for load in loads:
-        load.wait()
-
+    loads[0].wait()
     pl.semaphore_wait(barrier, len(greeted))
 
     halos = []
@@ -125,6 +123,8 @@
         )
         copy.start()
         halos.append(copy)
+    for load in loads[1:]:
+        load.wait()
 
     row = lax.broadcasted_iota(jnp.int32, (8, 2 * OWN), 0)
     lane = lax.broadcasted_iota(jnp.int32, (8, 2 * OWN), 1)
@@ -153,12 +153,13 @@
 
     norm_copies = []
 
-    def send_norms(step, devices):
+    def send_norms(step, devices, passed_on=None):
         copies = []
+        source = norms.at[step] if passed_on is None else norms_in.at[passed_on]
         for device in devices:
             i = len(norm_copies)
             copy = pltpu.make_async_remote_copy(
-                src_ref=norms.at[step], dst_ref=norms_in.at[i], send_sem=norm_send.at[i], recv_sem=norm_recv.at[i],
+                src_ref=source, dst_ref=norms_in.at[i], send_sem=norm_send.at[i], recv_sem=norm_recv.at[i],
                 device_id=device, device_id_type=MESH,
             )
             copy.start()
@@ -188,22 +189,35 @@
         taps = (-u * low1 * low2 / 6.0, up * low1 * low2 / 2.0, -up * u * low2 / 2.0, up * u * low1 / 6.0)
         weights.append([jnp.broadcast_to(w, (PATCHES, BLK)) for w in taps])
 
+    def tap_of(tile, r, place):
+        wide = jnp.broadcast_to(tile[r : r + 1], (PATCHES, BLK))
+        return jnp.take_along_axis(wide, place & (BLK - 1), axis=1)
+
+    middle = (strain[:, :BLK], strain[:, BLK:])
+    inner = {}
+    for block in range(2):
+        for r in range(4):
+            for m in range(4):
+                place = places[block] + m
+                inner[block, r, m] = jnp.where(
+                    place < (2 - block) * BLK, tap_of(middle[0], r, place), tap_of(middle[1], r, place)
+                )
+
+    add_norms(0, norms_c)
+    norms_z = send_norms(1, [at_z])
+
     for copy in halos:
         copy.wait()
-    before = jnp.where(linear == 0, 0.0, halo[0])
-    after = jnp.where(linear == n_all - 1, 0.0, halo[1])
-    tiles = [before, strain[:, :BLK], strain[:, BLK:], after]
+    ends = (jnp.where(linear == 0, 0.0, halo[0]), jnp.where(linear == n_all - 1, 0.0, halo[1]))
 
     for block in range(2):
         resampled = []
         for r in range(4):
-            wide = [jnp.broadcast_to(tiles[block + i][r : r + 1], (PATCHES, BLK)) for i in range(3)]
             total = None
             for m in range(4):
                 place = places[block] + m
-                within = place & (BLK - 1)
-                got = [jnp.take_along_axis(t, within, axis=1) for t in wide]
-                tap = jnp.where(place < BLK, got[0], jnp.where(place < 2 * BLK, got[1], got[2]))
+                outside = place < BLK if block == 0 else place >= 2 * BLK
+                tap = jnp.where(outside, tap_of(ends[block], r, place), inner[block, r, m])
                 term = weights[block][m] * tap
                 total = term if total is None else total + term
             resampled.append(total)
@@ -235,10 +249,11 @@
     coming[1, 0] = put(0, 0, at_y(-1))
     coming[-1, 0] = put(0, 0, at_y(1))
     coming[0, 1] = put(0, 0, at_z)
+    coming[1, 1] = put(0, 0, at_y(-1, 1))
+    coming[-1, 1] = put(0, 0, at_y(1, 1))
     sibling[0, 0] = put(0, 0, at_c)
-    add_norms(0, norms_c)
-    norms_z = send_norms(1, [at_z])
-
+    add_norms(1, norms_z)
+    norms_x = send_norms(2, [(tm_at(0, dx), spin) for dx in range(1, NX)])
     def landed_at(offset, z):
         coming[offset, z].wait_recv()
         if (offset, z) == (-2, 0):
@@ -249,7 +264,7 @@
             coming[4, 1] = put(2, 0, at_y(-2, 1))
             coming[3, 1] = put(2, 0, at_y(-1, 1))
             coming[3, 0] = put(2, 0, at_y(-1))
-        if z == 0 and abs(offset) <= 2:
+        if z == 0 and abs(offset) == 2:
             coming[offset, 1] = put(offset, 0, at_z)
         sibling[offset, z] = put(offset, z, at_c)
 
@@ -276,26 +291,28 @@
         acc[...] = acc[...] + product if multiplied else product
         multiplied.append(offset)
 
-    for offset, z in ((-2, 0), (2, 0), (-1, 0), (1, 0), (0, 1)):
+    early = ((-2, 0), (2, 0), (-1, 0), (1, 0), (0, 1), (-1, 1), (1, 1))
+    for offset, z in early:
         landed_at(offset, z)
-    add_norms(1, norms_z)
-    norms_x = send_norms(2, [(tm_at(0, dx), spin) for dx in range(1, NX)])
-    for offset, z in ((0, 0), (-2, 0), (2, 0), (-1, 0), (1, 0), (0, 1)):
+    for offset, z in ((0, 0),) + early[:3]:
         multiply(offset, z)
-    waiting = []
-    for pair in (((-2, 1), (2, 1)), ((-1, 1), (1, 1)), ((-3, 0), (3, 0)), ((-3, 1), (3, 1)), ((4, 0), (4, 1))):
-        for offset, z in pair:
+    add_norms(2, norms_x)
+    norms_zh = send_norms(3, [(tm_at(dz, 0), spin) for dz in (1, 3)])
+    for offset, z in early[3:]:
+        multiply(offset, z)
+    later = ((-3, 0), (3, 0), (-2, 1), (2, 1), (4, 0), (-3, 1), (3, 1), (4, 1))
+    for i in range(0, len(later), 2):
+        for offset, z in later[i : i + 2]:
             landed_at(offset, z)
-        if len(waiting) == 2:
-            add_norms(2, norms_x)
-            norms_zh = send_norms(3, [(tm_at(dz, 0), spin) for dz in range(1, NZ)])
-        for offset, z in waiting[-1:] and waiting[-1]:
-            multiply(offset, z)
-        waiting.append(pair)
-    for offset, z in waiting[-1]:
+        if i == 4:
+            add_norms(3, norms_zh)
+            norms_zh = send_norms(3, [(tm_at(1, 0), spin)], passed_on=norms_zh[0][0])
+        if i:
+            for offset, z in later[i - 2 : i]:
+                multiply(offset, z)
+    for offset, z in later[-2:]:
         multiply(offset, z)
-    add_norms(3, norms_zh)
-    norms_y = send_norms(4, [at_y(r) for r in range(1, NY)])
+    add_norms(4, norms_zh)
 
     step = (lax.broadcasted_iota(jnp.int32, (16, BLK), 0) * tm) % 16
     turn = step.astype(F32) / 16.0
@@ -320,6 +337,7 @@
         )
         copy.start()
         copies.append(copy)
+    norms_y = send_norms(5, [at_y(r) for r in range(1, NY)])
     spectrum(tm)
     for copy in started:
         copy.wait_send()
@@ -327,8 +345,8 @@
     for i in reversed(range(len(copies))):
         copies[i].wait_recv()
         total = total + landed[i]
-    add_norms(4, norms_y)
-    inverse = 1.0 / (norms[5, 0:1] + FLOOR)
+    add_norms(5, norms_y)
+    inverse = 1.0 / (norms[6, 0:1] + FLOOR)
     real, imag = total[:, 0:BLK], total[:, BLK:]
     power = (real * real + imag * imag) * inverse
     power = jnp.concatenate([power] * 8, axis=0).T
@@ -345,10 +363,11 @@
     return pl.pallas_call(
         kernel,
         out_shape=jax.ShapeDtypeStruct((4, PATCHES, NF // N_TM), F32),
-        in_specs=[anywhere] * 4 + [pl.BlockSpec(memory_space=pltpu.SMEM), anywhere],
+        in_specs=[anywhere] * 6,
         out_specs=pl.BlockSpec(memory_space=pltpu.VMEM),
         scratch_shapes=[
             pltpu.VMEM((4, OWN), F32),
+            pltpu.SMEM((4,), jnp.int32),
             pltpu.VMEM((2, 4, BLK), F32),
             pltpu.VMEM((PATCHES, 64), jnp.int32),
             pltpu.VMEM((PATCHES, 64), F32),
@@ -360,9 +379,9 @@
             pltpu.VMEM((2 * NF, 256), F32),
             pltpu.VMEM((N_TM, 16, 256), F32),
             pltpu.VMEM((N_TM - 1, 16, 256), F32),
-            pltpu.VMEM((6, 8, BLK), F32),
+            pltpu.VMEM((7, 8, BLK), F32),
             pltpu.VMEM((15, 8, BLK), F32),
-            dma((4,)), dma((NY,)), dma((2,)), dma((2,)), dma((31,)), dma((31,)),
+            dma((5,)), dma((NY,)), dma((2,)), dma((2,)), dma((31,)), dma((31,)),
             dma((15,)), dma((15,)), dma((15,)), dma((15,)),
         ],
         compiler_params=pltpu.CompilerParams(

time: 46.3 us -> 44.6 us (0.963)
  Pallas kernels: 44.7 us -> 43 us
    pallas_call x1, Pallas kernels: 44.7 us -> 43 us  [body(): pl.pallas_call(kernel, out_shape=jax.ShapeDtypeStruct((4, PATCHES, NF //...]
where the time goes in v4:
time: 44.6 us; the launch traced here: 44.4 us
  Pallas kernels  43 us (96%)
  local copies, waits for them, and re-layouts  1.38 us (3%)
    pallas_call x1, Pallas kernels, body(): pl.pallas_call(kernel, out_shape=jax.ShapeDtypeStruct((4, PATCHES, NF //...  43 us
    unnamed x1, local copies, waits for them, and re-layouts  1.38 us

profile of v4, /device:TPU:1, one launch (start us, length us, event | category | flops | bytes accessed | tf_op | source)
XLA Modules:
  0.0 44.4 jit_solution(8888835089283630639)
XLA Ops:
  0.0 43.0 %search.1 = f32[4,16,16]{2,1,0:T(8,128)} custom-call(f32[4,256]{1,0:T(4,128)} %strain_in.1, s32[16,64]{1,0:T(8,128)} %start_in.1, f32[16,64]{1,0:T(8,128)} %frac_in.1, f32[2,16,2,256]{3,2,1,0:T(2,128)} %antenna_in.1, s32[4]{0:T(128)} %spin_in.1, bf16[16,512,512]{2,1,0:T(8,128)(2,1)} %constant.2.clone.table_in), custom_call_target="tpu_custom_call" | custom-call | tf_op jit(solution)/shard_map/search/pallas_call | solution.py:363
  43.0 1.4 %copy.8 = f32[4,16,16]{2,1,0:T(8,128)} copy(f32[4,16,16]{2,1,0:T(8,128)} %search.1) | data formatting | bytes 8192

commit v5 on v4

--- a/solution.py
+++ b/solution.py
@@ -64,7 +64,7 @@
 def kernel(
     strain_in, start_in, frac_in, antenna_in, spin_in, table_in, out_ref,
     strain, spin_ref, halo, start, frac, antenna, table, turns, pieces, demod, acc, sums, landed, norms, norms_in,
-    in_sems, table_sems, halo_send, halo_recv, send, recv, sum_send, sum_recv, norm_send, norm_recv,
+    in_sems, table_sems, halo_send, halo_recv, send, recv, sum_send, sum_recv, norm_send, norm_recv, group_sems,
 ):
     tm, spin = lax.axis_index("tm"), lax.axis_index("spin")
     zl, y, c = spin // 16, (spin // 2) % NY, spin % 2
@@ -123,6 +123,9 @@
         )
         copy.start()
         halos.append(copy)
+    ahead, behind = (tm_at(1, 0), spin), (tm_at(3, 0), spin)
+    pl.semaphore_signal(group_sems.at[0], inc=1, device_id=ahead, device_id_type=MESH)
+    pl.semaphore_signal(group_sems.at[1], inc=1, device_id=behind, device_id_type=MESH)
     for load in loads[1:]:
         load.wait()
 
@@ -153,13 +156,12 @@
 
     norm_copies = []
 
-    def send_norms(step, devices, passed_on=None):
+    def send_norms(step, devices):
         copies = []
-        source = norms.at[step] if passed_on is None else norms_in.at[passed_on]
         for device in devices:
             i = len(norm_copies)
             copy = pltpu.make_async_remote_copy(
-                src_ref=source, dst_ref=norms_in.at[i], send_sem=norm_send.at[i], recv_sem=norm_recv.at[i],
+                src_ref=norms.at[step], dst_ref=norms_in.at[i], send_sem=norm_send.at[i], recv_sem=norm_recv.at[i],
                 device_id=device, device_id_type=MESH,
             )
             copy.start()
@@ -296,23 +298,24 @@
         landed_at(offset, z)
     for offset, z in ((0, 0),) + early[:3]:
         multiply(offset, z)
-    add_norms(2, norms_x)
-    norms_zh = send_norms(3, [(tm_at(dz, 0), spin) for dz in (1, 3)])
+    pl.semaphore_wait(group_sems.at[0], 1)
+    pl.semaphore_signal(group_sems.at[2], inc=1, device_id=ahead, device_id_type=MESH)
     for offset, z in early[3:]:
         multiply(offset, z)
     later = ((-3, 0), (3, 0), (-2, 1), (2, 1), (4, 0), (-3, 1), (3, 1), (4, 1))
     for i in range(0, len(later), 2):
         for offset, z in later[i : i + 2]:
             landed_at(offset, z)
-        if i == 4:
-            add_norms(3, norms_zh)
-            norms_zh = send_norms(3, [(tm_at(1, 0), spin)], passed_on=norms_zh[0][0])
+        if i == 2:
+            add_norms(2, norms_x)
+            pl.semaphore_wait(group_sems.at[1], 1)
+            pl.semaphore_wait(group_sems.at[2], 1)
+            norms_zh = send_norms(3, [(tm_at(dz, 0), spin) for dz in (2, 1, 3)])
         if i:
             for offset, z in later[i - 2 : i]:
                 multiply(offset, z)
     for offset, z in later[-2:]:
         multiply(offset, z)
-    add_norms(4, norms_zh)
 
     step = (lax.broadcasted_iota(jnp.int32, (16, BLK), 0) * tm) % 16
     turn = step.astype(F32) / 16.0
@@ -337,7 +340,8 @@
         )
         copy.start()
         copies.append(copy)
-    norms_y = send_norms(5, [at_y(r) for r in range(1, NY)])
+    add_norms(3, norms_zh)
+    norms_y = send_norms(4, [at_y(r) for r in range(1, NY)])
     spectrum(tm)
     for copy in started:
         copy.wait_send()
@@ -345,8 +349,8 @@
     for i in reversed(range(len(copies))):
         copies[i].wait_recv()
         total = total + landed[i]
-    add_norms(5, norms_y)
-    inverse = 1.0 / (norms[6, 0:1] + FLOOR)
+    add_norms(4, norms_y)
+    inverse = 1.0 / (norms[5, 0:1] + FLOOR)
     real, imag = total[:, 0:BLK], total[:, BLK:]
     power = (real * real + imag * imag) * inverse
     power = jnp.concatenate([power] * 8, axis=0).T
@@ -379,10 +383,11 @@
             pltpu.VMEM((2 * NF, 256), F32),
             pltpu.VMEM((N_TM, 16, 256), F32),
             pltpu.VMEM((N_TM - 1, 16, 256), F32),
-            pltpu.VMEM((7, 8, BLK), F32),
+            pltpu.VMEM((6, 8, BLK), F32),
             pltpu.VMEM((15, 8, BLK), F32),
             dma((5,)), dma((NY,)), dma((2,)), dma((2,)), dma((31,)), dma((31,)),
             dma((15,)), dma((15,)), dma((15,)), dma((15,)),
+            pltpu.SemaphoreType.REGULAR((3,)),
         ],
         compiler_params=pltpu.CompilerParams(
             collective_id=0, has_side_effects=True, vmem_limit_bytes=60 * 2**20

time: 44.6 us -> 43.9 us (0.984)
  Pallas kernels: 43 us -> 42.3 us
    pallas_call x1, Pallas kernels: 43 us -> 42.3 us  [body(): pl.pallas_call(kernel, out_shape=jax.ShapeDtypeStruct((4, PATCHES, NF //...]
where the time goes in v5:
time: 43.9 us; the launch traced here: 43.7 us
  Pallas kernels  42.3 us (96%)
  local copies, waits for them, and re-layouts  1.38 us (3%)
    pallas_call x1, Pallas kernels, body(): pl.pallas_call(kernel, out_shape=jax.ShapeDtypeStruct((4, PATCHES, NF //...  42.3 us
    unnamed x1, local copies, waits for them, and re-layouts  1.38 us

profile of v5, /device:TPU:1, one launch (start us, length us, event | category | flops | bytes accessed | tf_op | source)
XLA Modules:
  0.0 43.7 jit_solution(12998416599517650548)
XLA Ops:
  0.0 42.3 %search.1 = f32[4,16,16]{2,1,0:T(8,128)} custom-call(f32[4,256]{1,0:T(4,128)} %strain_in.1, s32[16,64]{1,0:T(8,128)} %start_in.1, f32[16,64]{1,0:T(8,128)} %frac_in.1, f32[2,16,2,256]{3,2,1,0:T(2,128)} %antenna_in.1, s32[4]{0:T(128)} %spin_in.1, bf16[16,512,512]{2,1,0:T(8,128)(2,1)} %constant.2.clone.table_in), custom_call_target="tpu_custom_call" | custom-call | tf_op jit(solution)/shard_map/search/pallas_call | solution.py:367
  42.3 1.4 %copy.8 = f32[4,16,16]{2,1,0:T(8,128)} copy(f32[4,16,16]{2,1,0:T(8,128)} %search.1) | data formatting | bytes 8192

commit v6 on v5

--- a/solution.py
+++ b/solution.py
@@ -92,8 +92,7 @@
         pltpu.make_async_copy(antenna_in, antenna, in_sems.at[3]),
         pltpu.make_async_copy(spin_in, spin_ref, in_sems.at[4]),
     ]
-    for load in loads:
-        load.start()
+    loads[0].start()
 
     barrier = pltpu.get_barrier_semaphore()
     shifts = [(dz, dx) for dz in (2, 1, 3, 0) for dx in (2, 1, 3, 0) if dz or dx]
@@ -101,15 +100,6 @@
     greeted += [(tm_at(0, dx), spin) for dx in (1, 2, 3)] + [(tm_at(dz, 0), spin) for dz in (1, 3)]
     for device in greeted:
         pl.semaphore_signal(barrier, inc=1, device_id=device, device_id_type=MESH)
-
-    offsets = (0, -1, 1, -2, 2, -3, 3, 4)
-    order = [(y + o + NY) % NY for o in offsets]
-    table_loads = []
-    for i, group in enumerate(order):
-        both = pl.ds(2 * group, 2)
-        load = pltpu.make_async_copy(table_in.at[both], table.at[both], table_sems.at[i])
-        load.start()
-        table_loads.append(load)
 
     loads[0].wait()
     pl.semaphore_wait(barrier, len(greeted))
@@ -126,6 +116,16 @@
     ahead, behind = (tm_at(1, 0), spin), (tm_at(3, 0), spin)
     pl.semaphore_signal(group_sems.at[0], inc=1, device_id=ahead, device_id_type=MESH)
     pl.semaphore_signal(group_sems.at[1], inc=1, device_id=behind, device_id_type=MESH)
+    for load in loads[1:]:
+        load.start()
+    offsets = (0, -1, 1, -2, 2, -3, 3, 4)
+    order = [(y + o + NY) % NY for o in offsets]
+    table_loads = []
+    for i, group in enumerate(order):
+        both = pl.ds(2 * group, 2)
+        load = pltpu.make_async_copy(table_in.at[both], table.at[both], table_sems.at[i])
+        load.start()
+        table_loads.append(load)
     for load in loads[1:]:
         load.wait()
 
@@ -349,15 +349,16 @@
     for i in reversed(range(len(copies))):
         copies[i].wait_recv()
         total = total + landed[i]
-    add_norms(4, norms_y)
+        if i == 4:
+            add_norms(4, norms_y)
+            for copy in copies + norm_copies:
+                copy.wait_send()
     inverse = 1.0 / (norms[5, 0:1] + FLOOR)
     real, imag = total[:, 0:BLK], total[:, BLK:]
     power = (real * real + imag * imag) * inverse
     power = jnp.concatenate([power] * 8, axis=0).T
     for s in range(4):
         out_ref[s] = power[s * 32 : s * 32 + 16, 0:16] + power[s * 32 + 16 : s * 32 + 32, 0:16]
-    for copy in copies + norm_copies:
-        copy.wait_send()
 
 
 def body(strain, stencil_start, stencil_frac, antenna, spin_index):

time: 43.9 us -> 44 us (level)
  no operation moved by 1% of the time
where the time goes in v6:
time: 44 us; the launch traced here: 43.7 us
  Pallas kernels  42.4 us (96%)
  local copies, waits for them, and re-layouts  1.38 us (3%)
    pallas_call x1, Pallas kernels, body(): pl.pallas_call(kernel, out_shape=jax.ShapeDtypeStruct((4, PATCHES, NF //...  42.4 us
    unnamed x1, local copies, waits for them, and re-layouts  1.38 us

profile of v6, /device:TPU:1, one launch (start us, length us, event | category | flops | bytes accessed | tf_op | source)
XLA Modules:
  0.0 43.7 jit_solution(12090780301851059714)
XLA Ops:
  0.0 42.4 %search.1 = f32[4,16,16]{2,1,0:T(8,128)} custom-call(f32[4,256]{1,0:T(4,128)} %strain_in.1, s32[16,64]{1,0:T(8,128)} %start_in.1, f32[16,64]{1,0:T(8,128)} %frac_in.1, f32[2,16,2,256]{3,2,1,0:T(2,128)} %antenna_in.1, s32[4]{0:T(128)} %spin_in.1, bf16[16,512,512]{2,1,0:T(8,128)(2,1)} %constant.2.clone.table_in), custom_call_target="tpu_custom_call" | custom-call | tf_op jit(solution)/shard_map/search/pallas_call | solution.py:368
  42.4 1.4 %copy.8 = f32[4,16,16]{2,1,0:T(8,128)} copy(f32[4,16,16]{2,1,0:T(8,128)} %search.1) | data formatting | bytes 8192

commit v7 on v6

--- a/solution.py
+++ b/solution.py
@@ -367,7 +367,7 @@
     dma = pltpu.SemaphoreType.DMA
     return pl.pallas_call(
         kernel,
-        out_shape=jax.ShapeDtypeStruct((4, PATCHES, NF // N_TM), F32),
+        out_shape=pltpu.VMEM((4, PATCHES, NF // N_TM), F32),
         in_specs=[anywhere] * 6,
         out_specs=pl.BlockSpec(memory_space=pltpu.VMEM),
         scratch_shapes=[

time: 44 us -> 42.5 us (0.966)
  local copies, waits for them, and re-layouts: 1.38 us -> 0.62 us
  Pallas kernels: 42.4 us -> 41.8 us
    unnamed x1, local copies, waits for them, and re-layouts: 1.38 us -> 0.62 us
    pallas_call x1, Pallas kernels: 42.4 us -> 41.8 us  [body(): pl.pallas_call(kernel, out_shape=pltpu.VMEM((4, PATCHES, NF // N_TM), F32...]
where the time goes in v7:
time: 42.5 us; the launch traced here: 42.4 us
  Pallas kernels  41.8 us (98%)
  local copies, waits for them, and re-layouts  0.62 us (1%)
    pallas_call x1, Pallas kernels, body(): pl.pallas_call(kernel, out_shape=pltpu.VMEM((4, PATCHES, NF // N_TM), F32...  41.8 us

profile of v7, /device:TPU:1, one launch (start us, length us, event | category | flops | bytes accessed | tf_op | source)
XLA Modules:
  0.0 42.4 jit_solution(9351565838718225118)
XLA Ops:
  0.0 41.8 %search.1 = f32[4,16,16]{2,1,0:T(8,128)S(1)} custom-call(f32[4,256]{1,0:T(4,128)} %strain_in.1, s32[16,64]{1,0:T(8,128)} %start_in.1, f32[16,64]{1,0:T(8,128)} %frac_in.1, f32[2,16,2,256]{3,2,1,0:T(2,128)} %antenna_in.1, s32[4]{0:T(128)} %spin_in.1, bf16[16,512,512]{2,1,0:T(8,128)(2,1)} %constant.2.clone.table_in), custom_call_target="tpu_custom_call" | custom-call | tf_op jit(solution)/shard_map/search/pallas_call | solution.py:368
  41.8 0.6 %copy.8 = f32[4,16,16]{2,1,0:T(8,128)} copy(f32[4,16,16]{2,1,0:T(8,128)S(1)} %search.1) | data formatting | bytes 8192

commit v8 on v7

--- a/solution.py
+++ b/solution.py
@@ -76,8 +76,9 @@
         other = (linear + offset + n_all) % n_all
         return (other // N_SPIN, other % N_SPIN)
 
-    def at_y(offset, z=0):
-        return (tm, (zl if z == 0 else 1 - zl) * 16 + ((y + offset + NY) % NY) * 2 + c)
+    def at_y(offset, z=0, core=0):
+        core = c if core == 0 else 1 - c
+        return (tm, (zl if z == 0 else 1 - zl) * 16 + ((y + offset + NY) % NY) * 2 + core)
 
     def tm_at(dz, dx):
         return ((zh + dz) % NZ) * NX + (x + dx) % NX
@@ -97,7 +98,7 @@
     barrier = pltpu.get_barrier_semaphore()
     shifts = [(dz, dx) for dz in (2, 1, 3, 0) for dx in (2, 1, 3, 0) if dz or dx]
     greeted = [along(1), along(-1), at_c] + [at_y(r) for r in (1, -1, 2, -2)] + [at_y(r, 1) for r in (0, 1, -1, 2)]
-    greeted += [(tm_at(0, dx), spin) for dx in (1, 2, 3)] + [(tm_at(dz, 0), spin) for dz in (1, 3)]
+    greeted += [at_y(2, 1, 1)] + [(tm_at(0, dx), spin) for dx in (1, 2, 3)] + [(tm_at(dz, 0), spin) for dz in (1, 3)]
     for device in greeted:
         pl.semaphore_signal(barrier, inc=1, device_id=device, device_id_type=MESH)
 
@@ -263,12 +264,14 @@
             coming[-3, 1] = put(-2, 0, at_y(1, 1))
             coming[-3, 0] = put(-2, 0, at_y(1))
         if (offset, z) == (2, 0):
+            sibling[4, 1] = put(2, 0, at_y(-2, 1, 1))
             coming[4, 1] = put(2, 0, at_y(-2, 1))
             coming[3, 1] = put(2, 0, at_y(-1, 1))
             coming[3, 0] = put(2, 0, at_y(-1))
         if z == 0 and abs(offset) == 2:
             coming[offset, 1] = put(offset, 0, at_z)
-        sibling[offset, z] = put(offset, z, at_c)
+        if (offset, z) != (4, 1):
+            sibling[offset, z] = put(offset, z, at_c)
 
     multiplied = []
 
@@ -356,7 +359,7 @@
     inverse = 1.0 / (norms[5, 0:1] + FLOOR)
     real, imag = total[:, 0:BLK], total[:, BLK:]
     power = (real * real + imag * imag) * inverse
-    power = jnp.concatenate([power] * 8, axis=0).T
+    power = power.T
     for s in range(4):
         out_ref[s] = power[s * 32 : s * 32 + 16, 0:16] + power[s * 32 + 16 : s * 32 + 32, 0:16]
 

time: 42.5 us -> 43.3 us (1.019)
  Pallas kernels: 41.8 us -> 42.5 us
    pallas_call x1, Pallas kernels: 41.8 us -> 42.5 us  [body(): pl.pallas_call(kernel, out_shape=pltpu.VMEM((4, PATCHES, NF // N_TM), F32...]
where the time goes in v8:
time: 43.3 us; the launch traced here: 43.1 us
  Pallas kernels  42.5 us (98%)
  local copies, waits for them, and re-layouts  0.62 us (1%)
    pallas_call x1, Pallas kernels, body(): pl.pallas_call(kernel, out_shape=pltpu.VMEM((4, PATCHES, NF // N_TM), F32...  42.5 us

profile of v8, /device:TPU:1, one launch (start us, length us, event | category | flops | bytes accessed | tf_op | source)
XLA Modules:
  0.0 43.1 jit_solution(4300984902578673895)
XLA Ops:
  0.0 42.5 %search.1 = f32[4,16,16]{2,1,0:T(8,128)S(1)} custom-call(f32[4,256]{1,0:T(4,128)} %strain_in.1, s32[16,64]{1,0:T(8,128)} %start_in.1, f32[16,64]{1,0:T(8,128)} %frac_in.1, f32[2,16,2,256]{3,2,1,0:T(2,128)} %antenna_in.1, s32[4]{0:T(128)} %spin_in.1, bf16[16,512,512]{2,1,0:T(8,128)(2,1)} %constant.2.clone.table_in), custom_call_target="tpu_custom_call" | custom-call | tf_op jit(solution)/shard_map/search/pallas_call | solution.py:371
  42.5 0.6 %copy.8 = f32[4,16,16]{2,1,0:T(8,128)} copy(f32[4,16,16]{2,1,0:T(8,128)S(1)} %search.1) | data formatting | bytes 8192

commit v9 on v7

--- a/solution.py
+++ b/solution.py
@@ -96,7 +96,7 @@
 
     barrier = pltpu.get_barrier_semaphore()
     shifts = [(dz, dx) for dz in (2, 1, 3, 0) for dx in (2, 1, 3, 0) if dz or dx]
-    greeted = [along(1), along(-1), at_c] + [at_y(r) for r in (1, -1, 2, -2)] + [at_y(r, 1) for r in (0, 1, -1, 2)]
+    greeted = [along(1), along(-1), at_c] + [at_y(r) for r in (1, -1, 2, -2)] + [at_y(r, 1) for r in (0, 1, -1, 2, -2)]
     greeted += [(tm_at(0, dx), spin) for dx in (1, 2, 3)] + [(tm_at(dz, 0), spin) for dz in (1, 3)]
     for device in greeted:
         pl.semaphore_signal(barrier, inc=1, device_id=device, device_id_type=MESH)
@@ -254,6 +254,8 @@
     coming[1, 1] = put(0, 0, at_y(-1, 1))
     coming[-1, 1] = put(0, 0, at_y(1, 1))
     sibling[0, 0] = put(0, 0, at_c)
+    coming[2, 1] = put(0, 0, at_y(-2, 1))
+    coming[-2, 1] = put(0, 0, at_y(2, 1))
     add_norms(1, norms_z)
     norms_x = send_norms(2, [(tm_at(0, dx), spin) for dx in range(1, NX)])
     def landed_at(offset, z):
@@ -266,8 +268,6 @@
             coming[4, 1] = put(2, 0, at_y(-2, 1))
             coming[3, 1] = put(2, 0, at_y(-1, 1))
             coming[3, 0] = put(2, 0, at_y(-1))
-        if z == 0 and abs(offset) == 2:
-            coming[offset, 1] = put(offset, 0, at_z)
         sibling[offset, z] = put(offset, z, at_c)
 
     multiplied = []
@@ -302,7 +302,7 @@
     pl.semaphore_signal(group_sems.at[2], inc=1, device_id=ahead, device_id_type=MESH)
     for offset, z in early[3:]:
         multiply(offset, z)
-    later = ((-3, 0), (3, 0), (-2, 1), (2, 1), (4, 0), (-3, 1), (3, 1), (4, 1))
+    later = ((-2, 1), (2, 1), (-3, 0), (3, 0), (4, 0), (-3, 1), (3, 1), (4, 1))
     for i in range(0, len(later), 2):
         for offset, z in later[i : i + 2]:
             landed_at(offset, z)
@@ -356,7 +356,7 @@
     inverse = 1.0 / (norms[5, 0:1] + FLOOR)
     real, imag = total[:, 0:BLK], total[:, BLK:]
     power = (real * real + imag * imag) * inverse
-    power = jnp.concatenate([power] * 8, axis=0).T
+    power = power.T
     for s in range(4):
         out_ref[s] = power[s * 32 : s * 32 + 16, 0:16] + power[s * 32 + 16 : s * 32 + 32, 0:16]
 

time: 42.5 us -> 42.8 us (level)
  no operation moved by 1% of the time
where the time goes in v9:
time: 42.8 us; the launch traced here: 42.7 us
  Pallas kernels  42.1 us (98%)
  local copies, waits for them, and re-layouts  0.62 us (1%)
    pallas_call x1, Pallas kernels, body(): pl.pallas_call(kernel, out_shape=pltpu.VMEM((4, PATCHES, NF // N_TM), F32...  42.1 us

profile of v9, /device:TPU:1, one launch (start us, length us, event | category | flops | bytes accessed | tf_op | source)
XLA Modules:
  0.0 42.7 jit_solution(2056180697086847451)
XLA Ops:
  0.0 42.1 %search.1 = f32[4,16,16]{2,1,0:T(8,128)S(1)} custom-call(f32[4,256]{1,0:T(4,128)} %strain_in.1, s32[16,64]{1,0:T(8,128)} %start_in.1, f32[16,64]{1,0:T(8,128)} %frac_in.1, f32[2,16,2,256]{3,2,1,0:T(2,128)} %antenna_in.1, s32[4]{0:T(128)} %spin_in.1, bf16[16,512,512]{2,1,0:T(8,128)(2,1)} %constant.2.clone.table_in), custom_call_target="tpu_custom_call" | custom-call | tf_op jit(solution)/shard_map/search/pallas_call | solution.py:368
  42.1 0.6 %copy.8 = f32[4,16,16]{2,1,0:T(8,128)} copy(f32[4,16,16]{2,1,0:T(8,128)S(1)} %search.1) | data formatting | bytes 8192

commit v10 on v9

--- a/solution.py
+++ b/solution.py
@@ -331,28 +331,45 @@
         sums[to, :, BLK:] = imag * cosine - real * sine
 
     copies = []
-    for i, (dz, dx) in enumerate(shifts):
-        to = tm_at(dz, dx)
-        spectrum(to)
+
+    def hand(of, to):
+        i = len(copies)
         copy = pltpu.make_async_remote_copy(
-            src_ref=sums.at[to], dst_ref=landed.at[i], send_sem=sum_send.at[i], recv_sem=sum_recv.at[i],
+            src_ref=sums.at[of], dst_ref=landed.at[i], send_sem=sum_send.at[i], recv_sem=sum_recv.at[i],
             device_id=(to, spin), device_id_type=MESH,
         )
         copy.start()
         copies.append(copy)
+
+    for dx in (2, 1, 3):
+        spectrum(tm_at(2, dx))
+        hand(tm_at(2, dx), tm_at(0, dx))
+    for dz, dx in shifts:
+        if dz != 2:
+            spectrum(tm_at(dz, dx))
+            hand(tm_at(dz, dx), tm_at(dz, dx))
+    far = tm_at(2, 0)
+    spectrum(far)
+    spectrum(tm)
+    passed = sums[far]
+    for i in range(3):
+        copies[i].wait_recv()
+        passed = passed + landed[i]
+    sums[far] = passed
+    hand(far, far)
     add_norms(3, norms_zh)
     norms_y = send_norms(4, [at_y(r) for r in range(1, NY)])
-    spectrum(tm)
     for copy in started:
         copy.wait_send()
     total = sums[tm]
-    for i in reversed(range(len(copies))):
+    for i in reversed(range(3, 14)):
         copies[i].wait_recv()
         total = total + landed[i]
-        if i == 4:
-            add_norms(4, norms_y)
-            for copy in copies + norm_copies:
-                copy.wait_send()
+    add_norms(4, norms_y)
+    for copy in copies + norm_copies:
+        copy.wait_send()
+    copies[14].wait_recv()
+    total = total + landed[14]
     inverse = 1.0 / (norms[5, 0:1] + FLOOR)
     real, imag = total[:, 0:BLK], total[:, BLK:]
     power = (real * real + imag * imag) * inverse

time: 42.8 us -> 41.7 us (0.974)
  Pallas kernels: 42.1 us -> 40.6 us
    pallas_call x1, Pallas kernels: 42.1 us -> 40.6 us  [body(): pl.pallas_call(kernel, out_shape=pltpu.VMEM((4, PATCHES, NF // N_TM), F32...]
where the time goes in v10:
time: 41.7 us; the launch traced here: 41.2 us
  Pallas kernels  40.6 us (97%)
  local copies, waits for them, and re-layouts  0.62 us (1%)
    pallas_call x1, Pallas kernels, body(): pl.pallas_call(kernel, out_shape=pltpu.VMEM((4, PATCHES, NF // N_TM), F32...  40.6 us

profile of v10, /device:TPU:1, one launch (start us, length us, event | category | flops | bytes accessed | tf_op | source)
XLA Modules:
  0.0 41.2 jit_solution(2992741885486612987)
XLA Ops:
  0.0 40.6 %search.1 = f32[4,16,16]{2,1,0:T(8,128)S(1)} custom-call(f32[4,256]{1,0:T(4,128)} %strain_in.1, s32[16,64]{1,0:T(8,128)} %start_in.1, f32[16,64]{1,0:T(8,128)} %frac_in.1, f32[2,16,2,256]{3,2,1,0:T(2,128)} %antenna_in.1, s32[4]{0:T(128)} %spin_in.1, bf16[16,512,512]{2,1,0:T(8,128)(2,1)} %constant.2.clone.table_in), custom_call_target="tpu_custom_call" | custom-call | tf_op jit(solution)/shard_map/search/pallas_call | solution.py:385
  40.6 0.6 %copy.8 = f32[4,16,16]{2,1,0:T(8,128)} copy(f32[4,16,16]{2,1,0:T(8,128)S(1)} %search.1) | data formatting | bytes 8192

commit v11 on v9

--- a/solution.py
+++ b/solution.py
@@ -95,7 +95,6 @@
     loads[0].start()
 
     barrier = pltpu.get_barrier_semaphore()
-    shifts = [(dz, dx) for dz in (2, 1, 3, 0) for dx in (2, 1, 3, 0) if dz or dx]
     greeted = [along(1), along(-1), at_c] + [at_y(r) for r in (1, -1, 2, -2)] + [at_y(r, 1) for r in (0, 1, -1, 2, -2)]
     greeted += [(tm_at(0, dx), spin) for dx in (1, 2, 3)] + [(tm_at(dz, 0), spin) for dz in (1, 3)]
     for device in greeted:
@@ -331,28 +330,42 @@
         sums[to, :, BLK:] = imag * cosine - real * sine
 
     copies = []
-    for i, (dz, dx) in enumerate(shifts):
-        to = tm_at(dz, dx)
-        spectrum(to)
+
+    def hand(of, to):
+        i = len(copies)
         copy = pltpu.make_async_remote_copy(
-            src_ref=sums.at[to], dst_ref=landed.at[i], send_sem=sum_send.at[i], recv_sem=sum_recv.at[i],
+            src_ref=sums.at[of], dst_ref=landed.at[i], send_sem=sum_send.at[i], recv_sem=sum_recv.at[i],
             device_id=(to, spin), device_id_type=MESH,
         )
         copy.start()
         copies.append(copy)
+
+    for dz in (2, 1, 3, 0):
+        for dx in (2, 1, 3):
+            spectrum(tm_at(dz, dx))
+            hand(tm_at(dz, dx), tm_at(0, dx))
+        spectrum(tm_at(dz, 0))
+    for group, dz in enumerate((2, 1, 3)):
+        far = tm_at(dz, 0)
+        passed = sums[far]
+        for i in range(3 * group, 3 * group + 3):
+            copies[i].wait_recv()
+            passed = passed + landed[i]
+        sums[far] = passed
+        hand(far, far)
     add_norms(3, norms_zh)
     norms_y = send_norms(4, [at_y(r) for r in range(1, NY)])
-    spectrum(tm)
     for copy in started:
         copy.wait_send()
     total = sums[tm]
-    for i in reversed(range(len(copies))):
+    for i in (9, 10, 11, 13, 14):
         copies[i].wait_recv()
         total = total + landed[i]
-        if i == 4:
-            add_norms(4, norms_y)
-            for copy in copies + norm_copies:
-                copy.wait_send()
+    add_norms(4, norms_y)
+    for copy in copies + norm_copies:
+        copy.wait_send()
+    copies[12].wait_recv()
+    total = total + landed[12]
     inverse = 1.0 / (norms[5, 0:1] + FLOOR)
     real, imag = total[:, 0:BLK], total[:, BLK:]
     power = (real * real + imag * imag) * inverse

time: 42.8 us -> 43 us (level); the launches traced: 42.7 us -> 42.3 us
  no operation moved by 1% of the time
where the time goes in v11:
time: 43 us; the launch traced here: 42.3 us
  Pallas kernels  41.7 us (97%)
  local copies, waits for them, and re-layouts  0.62 us (1%)
    pallas_call x1, Pallas kernels, body(): pl.pallas_call(kernel, out_shape=pltpu.VMEM((4, PATCHES, NF // N_TM), F32...  41.7 us

profile of v11, /device:TPU:1, one launch (start us, length us, event | category | flops | bytes accessed | tf_op | source)
XLA Modules:
  0.0 42.3 jit_solution(17450263593429780191)
XLA Ops:
  0.0 41.7 %search.1 = f32[4,16,16]{2,1,0:T(8,128)S(1)} custom-call(f32[4,256]{1,0:T(4,128)} %strain_in.1, s32[16,64]{1,0:T(8,128)} %start_in.1, f32[16,64]{1,0:T(8,128)} %frac_in.1, f32[2,16,2,256]{3,2,1,0:T(2,128)} %antenna_in.1, s32[4]{0:T(128)} %spin_in.1, bf16[16,512,512]{2,1,0:T(8,128)(2,1)} %constant.2.clone.table_in), custom_call_target="tpu_custom_call" | custom-call | tf_op jit(solution)/shard_map/search/pallas_call | solution.py:381
  41.7 0.6 %copy.8 = f32[4,16,16]{2,1,0:T(8,128)} copy(f32[4,16,16]{2,1,0:T(8,128)S(1)} %search.1) | data formatting | bytes 8192

commit v12 on v10

--- a/solution.py
+++ b/solution.py
@@ -95,7 +95,7 @@
     loads[0].start()
 
     barrier = pltpu.get_barrier_semaphore()
-    shifts = [(dz, dx) for dz in (2, 1, 3, 0) for dx in (2, 1, 3, 0) if dz or dx]
+    shifts = [(dz, dx) for dx in (2, 1, 3, 0) for dz in (2, 1, 3, 0) if dz or dx]
     greeted = [along(1), along(-1), at_c] + [at_y(r) for r in (1, -1, 2, -2)] + [at_y(r, 1) for r in (0, 1, -1, 2, -2)]
     greeted += [(tm_at(0, dx), spin) for dx in (1, 2, 3)] + [(tm_at(dz, 0), spin) for dz in (1, 3)]
     for device in greeted:

time: 41.7 us -> 41.7 us (level)
  no operation moved by 1% of the time
where the time goes in v12:
time: 41.7 us; the launch traced here: 41.2 us
  Pallas kernels  40.6 us (97%)
  local copies, waits for them, and re-layouts  0.62 us (1%)
    pallas_call x1, Pallas kernels, body(): pl.pallas_call(kernel, out_shape=pltpu.VMEM((4, PATCHES, NF // N_TM), F32...  40.6 us

profile of v12, /device:TPU:1, one launch (start us, length us, event | category | flops | bytes accessed | tf_op | source)
XLA Modules:
  0.0 41.2 jit_solution(5865910147183588419)
XLA Ops:
  0.0 40.6 %search.1 = f32[4,16,16]{2,1,0:T(8,128)S(1)} custom-call(f32[4,256]{1,0:T(4,128)} %strain_in.1, s32[16,64]{1,0:T(8,128)} %start_in.1, f32[16,64]{1,0:T(8,128)} %frac_in.1, f32[2,16,2,256]{3,2,1,0:T(2,128)} %antenna_in.1, s32[4]{0:T(128)} %spin_in.1, bf16[16,512,512]{2,1,0:T(8,128)(2,1)} %constant.2.clone.table_in), custom_call_target="tpu_custom_call" | custom-call | tf_op jit(solution)/shard_map/search/pallas_call | solution.py:385
  40.6 0.6 %copy.8 = f32[4,16,16]{2,1,0:T(8,128)} copy(f32[4,16,16]{2,1,0:T(8,128)S(1)} %search.1) | data formatting | bytes 8192
